TPU v7x, 32 devices: a whole 2x2x4 slice. The times are simulated.
32 devices in a mesh: domain: 8 (over z, x), group: 4 (over y, core).
Axes of the slice: x: 2, y: 2, z: 4, core: 2. Of those that a mesh axis runs over, the one named last changes fastest.
Arguments:
- centers: float32 [2048, 3], P(('domain', 'group')), may hold values from -24 to 24
- offsets: float32 [2048, 3, 144], P(('domain', 'group')), may hold values from -6 to 6
- density: float32 [2048, 3, 144], P(('domain', 'group')), may hold values from -6 to 6
- area: float32 [2048, 144], P(('domain', 'group')), may hold values from 0.03 to 0.3
- upsample: float32 [544, 144], replicated
- self_operator: float32 [144, 144], replicated, may hold values from -0.5 to 0.5
- near_sources: int32 [2048, 4], P(('domain', 'group')), may hold values from 0 to 2047, as said below
- near_counts: int32 [2048], P(('domain', 'group')), may hold values from 1 to 4, as said below
- leaf_slot: int32 [2048], P(('domain', 'group')), may hold values from 0 to 4095, as said below
- leaf_list: int32 [256, 8], P(('domain', 'group')), may hold values from 0 to 255
Outputs:
- velocity: float32 [2048, 3, 144], P(('domain', 'group'))
Inputs may be any that keep to these rules, and one draw needn't show every extreme that they name: `near_sources`: each near source lies in the target's own domain or in one of the two adjacent domains of 2048 / 8 vesicles, and is never the target itself; slots past the count hold valid indices too. `near_counts`: the first vesicle of every device has 4 live slots. `leaf_slot`: no two vesicles share a slot, and a vesicle's slot lies in a leaf block of a device of its own domain.
All inputs are finite; a program needn't handle non-finite values.
Results may differ from a plain program's by a relative error of at most 0.00014.
Values sent between devices are 32-bit elements; how exact they have to be, the bound alone decides.
No kernel may reach another device: no remote copies, remote signals or barrier semaphores. Data moves between devices by JAX's collectives and lax.ppermute only.
A program may use at most 128 MiB of HBM per device.

v0:
```python
import math

import jax
import jax.numpy as jnp
from jax import lax
from jax.sharding import PartitionSpec as P

LEAF_CAP = 16


BLOB2 = 0.25


def padded(cells, sides, width):
    for axis, dim in sides:
        count = lax.axis_size(axis)
        ends = count - 1
        head = lax.slice_in_dim(cells, 0, width, axis=dim)
        tail = lax.slice_in_dim(cells, cells.shape[dim] - width, cells.shape[dim], axis=dim)
        cells = jnp.concatenate(
            [
                lax.ppermute(tail, axis, [(i, (i + 1) % count) for i in range(ends)]),
                cells,
                lax.ppermute(head, axis, [((i + 1) % count, i) for i in range(ends)]),
            ],
            axis=dim,
        )
    return cells


def stokes(rel, force):
    dist = jnp.sum(rel * rel, axis=0) + BLOB2
    inverse = 1.0 / (dist * jnp.sqrt(dist))
    project = jnp.sum(rel * force, axis=0)
    return jnp.sum(inverse * ((dist + BLOB2) * force + project * rel), axis=-1)


def near_block(targets, sources):
    rel = targets[:, :, None, :, None] - sources[:3, :, :, None, :]
    return jnp.sum(stokes(rel, sources[3:, :, :, None, :]), axis=2)


def shards(
    centers,
    offsets,
    density,
    area,
    upsample,
    self_operator,
    near_sources,
    near_counts,
    leaf_slot,
    leaf_list,
):
    highest = lax.Precision.HIGHEST
    rows = centers.shape[0]
    points = offsets.shape[2]
    groups = lax.axis_size("group")
    domain = lax.axis_index("domain")
    grid = offsets + centers[:, :, None]
    weighted = density * area[:, None, :]
    coarse = jnp.concatenate([grid, weighted], axis=1)
    source_domain = near_sources // (groups * rows)
    source_group = near_sources // rows % groups
    source_local = near_sources % rows
    domain_step = source_domain - domain + 1
    rimmed = padded(coarse, (("domain", 0),), rows)
    pool = lax.all_gather(rimmed, "group", axis=0, tiled=True)
    position = source_group * (3 * rows) + domain_step * rows + source_local
    self_term = jnp.einsum("ip,vcp->vci", self_operator, density, precision=highest)
    slots_each = near_sources.shape[1]
    live = (lax.broadcasted_iota(jnp.int32, near_sources.shape, 1) < near_counts[:, None]).astype(
        jnp.float32
    )
    block = math.gcd(rows, 4)
    turns = rows // block

    def one_block(items):
        targets, spots, mask = items
        chosen = pool[spots]
        chosen = jnp.einsum("qp,bkcp->bkcq", upsample, chosen, precision=highest)
        picked = jnp.transpose(chosen, (2, 0, 1, 3))
        picked = jnp.concatenate([picked[:3], picked[3:] * mask[None, :, :, None]], axis=0)
        return near_block(jnp.transpose(targets, (1, 0, 2)), picked)

    near = lax.map(
        one_block,
        (
            grid.reshape(turns, block, 3, points),
            position.reshape(turns, block, slots_each),
            live.reshape(turns, block, slots_each),
        ),
    )
    near = jnp.transpose(near, (0, 2, 1, 3)).reshape(rows, 3, points)
    total = jnp.sum(weighted, axis=2)
    leaf_rows = leaf_list.shape[0]
    per_leaf = leaf_list.shape[1]
    capacity = LEAF_CAP
    own_slots = leaf_rows * capacity
    local_slot = leaf_slot - domain * (groups * own_slots)
    payload = jnp.transpose(jnp.concatenate([centers, total], axis=1))
    placed = jnp.zeros((6, groups * own_slots), jnp.float32).at[:, local_slot].set(payload)
    owned = lax.psum_scatter(placed, "group", scatter_dimension=1, tiled=True)
    everything = lax.all_gather(owned, ("domain", "group"), axis=1, tiled=True)
    spots = (
        leaf_list[:, :, None] * capacity + jnp.arange(capacity, dtype=jnp.int32)[None, None, :]
    ).reshape(leaf_rows, per_leaf * capacity)
    picked = everything[:, spots]
    targets = owned[:3].reshape(3, leaf_rows, capacity)
    rel = targets[:, :, :, None] - picked[:3, :, None, :]
    result = stokes(rel, picked[3:, :, None, :]).reshape(3, own_slots)
    returned = lax.all_gather(result, "group", axis=1, tiled=True)
    far = returned[:, local_slot]
    return self_term + near + jnp.transpose(far)[:, :, None]


def solution(mesh):
    in_specs = (
        P(("domain", "group"), None),
        P(("domain", "group"), None, None),
        P(("domain", "group"), None, None),
        P(("domain", "group"), None),
        P(),
        P(),
        P(("domain", "group"), None),
        P(("domain", "group")),
        P(("domain", "group")),
        P(("domain", "group"), None),
    )
    out_specs = P(("domain", "group"), None, None)
    return jax.shard_map(shards, mesh=mesh, in_specs=in_specs, out_specs=out_specs, check_vma=False)
```

profile of v0, /device:TPU:0, one launch (start us, length us, event | category | flops | bytes accessed | tf_op | source)
XLA Modules:
  0.0 529.1 jit_solution(15453720792935967597)
XLA Ops:
  8.7 4.9 collective-permute-start
  18.0 12.4 %collective-permute-done = f32[64,6,144]{2,0,1:T(8,128)S(1)} collective-permute-done((f32[64,6,144]{2,0,1:T(8,128)S(1)}, f32[64,6,144]{2,0,1:T(8,128)S(1)}, u32[]{:S(2)}, u32[]{:S(2)}) %collective-permute-start) | collective-permute-done | bytes 221216 | tf_op jit(solution)/shard_map/ppermute | solution.py:22
  33.0 7.5 %reduce-scatter.2.cloned.1.call-done = f32[6,128]{0,1:T(8,128)} async-done(((f32[6,512]{0,1:T(8,128)}), f32[6,128]{0,1:T(8,128)}) %reduce-scatter.2.cloned.1.call-update) | async-done | bytes 3088 | tf_op jit(solution)/shard_map/reduce_scatter | solution.py:103
  40.5 51.2 %all_gather.10 = f32[6,4096]{0,1:T(8,128)S(1)} all-gather(f32[6,128]{0,1:T(8,128)} %reduce-scatter.2.cloned.1.call-done), channel_id=1, replica_groups=mesh['domain'=8,'group'=4] {'domain','group'}, dimensions={1}, use_global_device_ids=true | all-gather | bytes 101376 | tf_op jit(solution)/shard_map/all_gather | solution.py:104
  96.6 7.8 %all_gather.11 = f32[3,512]{0,1:T(8,128)S(1)} all-gather(f32[3,128]{0,1:T(8,128)S(1)} %bitcast.62), channel_id=1, replica_groups=mesh['domain'=8,'group'=4] {'group'}, dimensions={1}, use_global_device_ids=true | all-gather | bytes 7680 | tf_op jit(solution)/shard_map/all_gather | solution.py:112
  106.7 413.5 %while.12 = (s32[]{:T(128)}, f32[16,3,4,144]{3,2,1,0:T(4,128)}, f32[16,4,3,144]{3,1,0,2:T(4,128)S(1)}, s32[16,4,4]{2,1,0:T(4,128)S(1)}, f32[768,6,144]{2,1,0:T(8...) while((s32[]{:T(128)}, f32[16,3,4,144]{3,2,1,0:T(4,128)}, ...), condition=%wide.region_4.5_spmd, body=%wide.region_0.4_spmd.sunk | while | flops 134136688 | bytes 62162620 | solution.py:86
  106.8 3.3 gather_fusion
  110.8 6.8 %fusion.43 = (f32[4,4,144,544]{3,2,1,0:T(8,128)S(1)}, f32[4,4,144,544]{3,2,1,0:T(8,128)}) fusion(f32[3,4,4,544]{3,2,1,0:T(4,128)S(1)} %copy.111, f32[3,4,144]{2,1,0:T(4,128)S(1)} %dynamic-slice_bitcast_fusion.5, f32[3,4,4,544]{3,2,1,0:T(4,128)S(1)} %copy.112), kind=kLoop, calls=%fused_computation.7.clone.1 | loop fusion | flops 16293888 | bytes 10242816 | tf_op jit(solution)/shard_map/while/body/eval_jaxpr/reduce_sum | solution.py:32
  117.6 6.3 %fusion.44 = (f32[4,4,144,544]{3,2,1,0:T(8,128)}, f32[4,4,144,544]{3,2,1,0:T(8,128)}) fusion(f32[4,4,144,544]{3,2,1,0:T(8,128)S(1)} %get-tuple-element.210), kind=kLoop, calls=%fused_computation.13.clone.1 | loop fusion | flops 5013504 | bytes 15040512 | tf_op jit(solution)/shard_map/while/body/eval_jaxpr/div | solution.py:33
  123.9 8.0 %fusion.45 = f32[3,4,144]{2,1,0:T(4,128)S(1)} fusion(f32[4,4,144,544]{3,2,1,0:T(8,128)S(1)} %copy-done.1, f32[3,4,4,544]{3,2,1,0:T(4,128)S(1)} %copy.112, f32[4,4,144,544]{3,2,1,0:T(8,128)} %get-tuple-element.211, f32[4,4,144,544]{3,2,1,0:T(8,128)} %get-tuple-element.212, f32[3,4,4,544]{3,2,1,0:T(4,128)S(1)} %copy.111, ...), kind=kLoop, calls=%fused_computation.11.clone.1 | loop fusion | flops 22559040 | bytes 15263232 | tf_op jit(solution)/shard_map/while/body/eval_jaxpr/reduce_sum | solution.py:40
  132.6 3.3 gather_fusion
  136.7 6.8 %fusion.43 = (f32[4,4,144,544]{3,2,1,0:T(8,128)S(1)}, f32[4,4,144,544]{3,2,1,0:T(8,128)}) fusion(f32[3,4,4,544]{3,2,1,0:T(4,128)S(1)} %copy.111, f32[3,4,144]{2,1,0:T(4,128)S(1)} %dynamic-slice_bitcast_fusion.5, f32[3,4,4,544]{3,2,1,0:T(4,128)S(1)} %copy.112), kind=kLoop, calls=%fused_computation.7.clone.1 | loop fusion | flops 16293888 | bytes 10242816 | tf_op jit(solution)/shard_map/while/body/eval_jaxpr/reduce_sum | solution.py:32
  143.4 6.3 %fusion.44 = (f32[4,4,144,544]{3,2,1,0:T(8,128)}, f32[4,4,144,544]{3,2,1,0:T(8,128)}) fusion(f32[4,4,144,544]{3,2,1,0:T(8,128)S(1)} %get-tuple-element.210), kind=kLoop, calls=%fused_computation.13.clone.1 | loop fusion | flops 5013504 | bytes 15040512 | tf_op jit(solution)/shard_map/while/body/eval_jaxpr/div | solution.py:33
  149.8 8.0 %fusion.45 = f32[3,4,144]{2,1,0:T(4,128)S(1)} fusion(f32[4,4,144,544]{3,2,1,0:T(8,128)S(1)} %copy-done.1, f32[3,4,4,544]{3,2,1,0:T(4,128)S(1)} %copy.112, f32[4,4,144,544]{3,2,1,0:T(8,128)} %get-tuple-element.211, f32[4,4,144,544]{3,2,1,0:T(8,128)} %get-tuple-element.212, f32[3,4,4,544]{3,2,1,0:T(4,128)S(1)} %copy.111, ...), kind=kLoop, calls=%fused_computation.11.clone.1 | loop fusion | flops 22559040 | bytes 15263232 | tf_op jit(solution)/shard_map/while/body/eval_jaxpr/reduce_sum | solution.py:40
  158.5 3.3 gather_fusion
  162.5 6.8 %fusion.43 = (f32[4,4,144,544]{3,2,1,0:T(8,128)S(1)}, f32[4,4,144,544]{3,2,1,0:T(8,128)}) fusion(f32[3,4,4,544]{3,2,1,0:T(4,128)S(1)} %copy.111, f32[3,4,144]{2,1,0:T(4,128)S(1)} %dynamic-slice_bitcast_fusion.5, f32[3,4,4,544]{3,2,1,0:T(4,128)S(1)} %copy.112), kind=kLoop, calls=%fused_computation.7.clone.1 | loop fusion | flops 16293888 | bytes 10242816 | tf_op jit(solution)/shard_map/while/body/eval_jaxpr/reduce_sum | solution.py:32
  169.3 6.3 %fusion.44 = (f32[4,4,144,544]{3,2,1,0:T(8,128)}, f32[4,4,144,544]{3,2,1,0:T(8,128)}) fusion(f32[4,4,144,544]{3,2,1,0:T(8,128)S(1)} %get-tuple-element.210), kind=kLoop, calls=%fused_computation.13.clone.1 | loop fusion | flops 5013504 | bytes 15040512 | tf_op jit(solution)/shard_map/while/body/eval_jaxpr/div | solution.py:33
  175.6 8.0 %fusion.45 = f32[3,4,144]{2,1,0:T(4,128)S(1)} fusion(f32[4,4,144,544]{3,2,1,0:T(8,128)S(1)} %copy-done.1, f32[3,4,4,544]{3,2,1,0:T(4,128)S(1)} %copy.112, f32[4,4,144,544]{3,2,1,0:T(8,128)} %get-tuple-element.211, f32[4,4,144,544]{3,2,1,0:T(8,128)} %get-tuple-element.212, f32[3,4,4,544]{3,2,1,0:T(4,128)S(1)} %copy.111, ...), kind=kLoop, calls=%fused_computation.11.clone.1 | loop fusion | flops 22559040 | bytes 15263232 | tf_op jit(solution)/shard_map/while/body/eval_jaxpr/reduce_sum | solution.py:40
  184.3 3.3 gather_fusion
  188.3 6.8 %fusion.43 = (f32[4,4,144,544]{3,2,1,0:T(8,128)S(1)}, f32[4,4,144,544]{3,2,1,0:T(8,128)}) fusion(f32[3,4,4,544]{3,2,1,0:T(4,128)S(1)} %copy.111, f32[3,4,144]{2,1,0:T(4,128)S(1)} %dynamic-slice_bitcast_fusion.5, f32[3,4,4,544]{3,2,1,0:T(4,128)S(1)} %copy.112), kind=kLoop, calls=%fused_computation.7.clone.1 | loop fusion | flops 16293888 | bytes 10242816 | tf_op jit(solution)/shard_map/while/body/eval_jaxpr/reduce_sum | solution.py:32
  195.1 6.3 %fusion.44 = (f32[4,4,144,544]{3,2,1,0:T(8,128)}, f32[4,4,144,544]{3,2,1,0:T(8,128)}) fusion(f32[4,4,144,544]{3,2,1,0:T(8,128)S(1)} %get-tuple-element.210), kind=kLoop, calls=%fused_computation.13.clone.1 | loop fusion | flops 5013504 | bytes 15040512 | tf_op jit(solution)/shard_map/while/body/eval_jaxpr/div | solution.py:33
  201.4 8.0 %fusion.45 = f32[3,4,144]{2,1,0:T(4,128)S(1)} fusion(f32[4,4,144,544]{3,2,1,0:T(8,128)S(1)} %copy-done.1, f32[3,4,4,544]{3,2,1,0:T(4,128)S(1)} %copy.112, f32[4,4,144,544]{3,2,1,0:T(8,128)} %get-tuple-element.211, f32[4,4,144,544]{3,2,1,0:T(8,128)} %get-tuple-element.212, f32[3,4,4,544]{3,2,1,0:T(4,128)S(1)} %copy.111, ...), kind=kLoop, calls=%fused_computation.11.clone.1 | loop fusion | flops 22559040 | bytes 15263232 | tf_op jit(solution)/shard_map/while/body/eval_jaxpr/reduce_sum | solution.py:40
  214.2 6.8 %fusion.43 = (f32[4,4,144,544]{3,2,1,0:T(8,128)S(1)}, f32[4,4,144,544]{3,2,1,0:T(8,128)}) fusion(f32[3,4,4,544]{3,2,1,0:T(4,128)S(1)} %copy.111, f32[3,4,144]{2,1,0:T(4,128)S(1)} %dynamic-slice_bitcast_fusion.5, f32[3,4,4,544]{3,2,1,0:T(4,128)S(1)} %copy.112), kind=kLoop, calls=%fused_computation.7.clone.1 | loop fusion | flops 16293888 | bytes 10242816 | tf_op jit(solution)/shard_map/while/body/eval_jaxpr/reduce_sum | solution.py:32
  220.9 6.3 %fusion.44 = (f32[4,4,144,544]{3,2,1,0:T(8,128)}, f32[4,4,144,544]{3,2,1,0:T(8,128)}) fusion(f32[4,4,144,544]{3,2,1,0:T(8,128)S(1)} %get-tuple-element.210), kind=kLoop, calls=%fused_computation.13.clone.1 | loop fusion | flops 5013504 | bytes 15040512 | tf_op jit(solution)/shard_map/while/body/eval_jaxpr/div | solution.py:33
  227.3 8.0 %fusion.45 = f32[3,4,144]{2,1,0:T(4,128)S(1)} fusion(f32[4,4,144,544]{3,2,1,0:T(8,128)S(1)} %copy-done.1, f32[3,4,4,544]{3,2,1,0:T(4,128)S(1)} %copy.112, f32[4,4,144,544]{3,2,1,0:T(8,128)} %get-tuple-element.211, f32[4,4,144,544]{3,2,1,0:T(8,128)} %get-tuple-element.212, f32[3,4,4,544]{3,2,1,0:T(4,128)S(1)} %copy.111, ...), kind=kLoop, calls=%fused_computation.11.clone.1 | loop fusion | flops 22559040 | bytes 15263232 | tf_op jit(solution)/shard_map/while/body/eval_jaxpr/reduce_sum | solution.py:40
  236.0 3.3 gather_fusion
  240.0 6.8 %fusion.43 = (f32[4,4,144,544]{3,2,1,0:T(8,128)S(1)}, f32[4,4,144,544]{3,2,1,0:T(8,128)}) fusion(f32[3,4,4,544]{3,2,1,0:T(4,128)S(1)} %copy.111, f32[3,4,144]{2,1,0:T(4,128)S(1)} %dynamic-slice_bitcast_fusion.5, f32[3,4,4,544]{3,2,1,0:T(4,128)S(1)} %copy.112), kind=kLoop, calls=%fused_computation.7.clone.1 | loop fusion | flops 16293888 | bytes 10242816 | tf_op jit(solution)/shard_map/while/body/eval_jaxpr/reduce_sum | solution.py:32
  246.8 6.3 %fusion.44 = (f32[4,4,144,544]{3,2,1,0:T(8,128)}, f32[4,4,144,544]{3,2,1,0:T(8,128)}) fusion(f32[4,4,144,544]{3,2,1,0:T(8,128)S(1)} %get-tuple-element.210), kind=kLoop, calls=%fused_computation.13.clone.1 | loop fusion | flops 5013504 | bytes 15040512 | tf_op jit(solution)/shard_map/while/body/eval_jaxpr/div | solution.py:33
  253.1 8.0 %fusion.45 = f32[3,4,144]{2,1,0:T(4,128)S(1)} fusion(f32[4,4,144,544]{3,2,1,0:T(8,128)S(1)} %copy-done.1, f32[3,4,4,544]{3,2,1,0:T(4,128)S(1)} %copy.112, f32[4,4,144,544]{3,2,1,0:T(8,128)} %get-tuple-element.211, f32[4,4,144,544]{3,2,1,0:T(8,128)} %get-tuple-element.212, f32[3,4,4,544]{3,2,1,0:T(4,128)S(1)} %copy.111, ...), kind=kLoop, calls=%fused_computation.11.clone.1 | loop fusion | flops 22559040 | bytes 15263232 | tf_op jit(solution)/shard_map/while/body/eval_jaxpr/reduce_sum | solution.py:40
  261.9 3.3 gather_fusion
  265.9 6.8 %fusion.43 = (f32[4,4,144,544]{3,2,1,0:T(8,128)S(1)}, f32[4,4,144,544]{3,2,1,0:T(8,128)}) fusion(f32[3,4,4,544]{3,2,1,0:T(4,128)S(1)} %copy.111, f32[3,4,144]{2,1,0:T(4,128)S(1)} %dynamic-slice_bitcast_fusion.5, f32[3,4,4,544]{3,2,1,0:T(4,128)S(1)} %copy.112), kind=kLoop, calls=%fused_computation.7.clone.1 | loop fusion | flops 16293888 | bytes 10242816 | tf_op jit(solution)/shard_map/while/body/eval_jaxpr/reduce_sum | solution.py:32
  272.6 6.3 %fusion.44 = (f32[4,4,144,544]{3,2,1,0:T(8,128)}, f32[4,4,144,544]{3,2,1,0:T(8,128)}) fusion(f32[4,4,144,544]{3,2,1,0:T(8,128)S(1)} %get-tuple-element.210), kind=kLoop, calls=%fused_computation.13.clone.1 | loop fusion | flops 5013504 | bytes 15040512 | tf_op jit(solution)/shard_map/while/body/eval_jaxpr/div | solution.py:33
  279.0 8.0 %fusion.45 = f32[3,4,144]{2,1,0:T(4,128)S(1)} fusion(f32[4,4,144,544]{3,2,1,0:T(8,128)S(1)} %copy-done.1, f32[3,4,4,544]{3,2,1,0:T(4,128)S(1)} %copy.112, f32[4,4,144,544]{3,2,1,0:T(8,128)} %get-tuple-element.211, f32[4,4,144,544]{3,2,1,0:T(8,128)} %get-tuple-element.212, f32[3,4,4,544]{3,2,1,0:T(4,128)S(1)} %copy.111, ...), kind=kLoop, calls=%fused_computation.11.clone.1 | loop fusion | flops 22559040 | bytes 15263232 | tf_op jit(solution)/shard_map/while/body/eval_jaxpr/reduce_sum | solution.py:40
  287.7 3.3 gather_fusion
  291.7 6.8 %fusion.43 = (f32[4,4,144,544]{3,2,1,0:T(8,128)S(1)}, f32[4,4,144,544]{3,2,1,0:T(8,128)}) fusion(f32[3,4,4,544]{3,2,1,0:T(4,128)S(1)} %copy.111, f32[3,4,144]{2,1,0:T(4,128)S(1)} %dynamic-slice_bitcast_fusion.5, f32[3,4,4,544]{3,2,1,0:T(4,128)S(1)} %copy.112), kind=kLoop, calls=%fused_computation.7.clone.1 | loop fusion | flops 16293888 | bytes 10242816 | tf_op jit(solution)/shard_map/while/body/eval_jaxpr/reduce_sum | solution.py:32
  298.5 6.3 %fusion.44 = (f32[4,4,144,544]{3,2,1,0:T(8,128)}, f32[4,4,144,544]{3,2,1,0:T(8,128)}) fusion(f32[4,4,144,544]{3,2,1,0:T(8,128)S(1)} %get-tuple-element.210), kind=kLoop, calls=%fused_computation.13.clone.1 | loop fusion | flops 5013504 | bytes 15040512 | tf_op jit(solution)/shard_map/while/body/eval_jaxpr/div | solution.py:33
  304.8 8.0 %fusion.45 = f32[3,4,144]{2,1,0:T(4,128)S(1)} fusion(f32[4,4,144,544]{3,2,1,0:T(8,128)S(1)} %copy-done.1, f32[3,4,4,544]{3,2,1,0:T(4,128)S(1)} %copy.112, f32[4,4,144,544]{3,2,1,0:T(8,128)} %get-tuple-element.211, f32[4,4,144,544]{3,2,1,0:T(8,128)} %get-tuple-element.212, f32[3,4,4,544]{3,2,1,0:T(4,128)S(1)} %copy.111, ...), kind=kLoop, calls=%fused_computation.11.clone.1 | loop fusion | flops 22559040 | bytes 15263232 | tf_op jit(solution)/shard_map/while/body/eval_jaxpr/reduce_sum | solution.py:40
  313.5 3.3 gather_fusion
  317.6 6.8 %fusion.43 = (f32[4,4,144,544]{3,2,1,0:T(8,128)S(1)}, f32[4,4,144,544]{3,2,1,0:T(8,128)}) fusion(f32[3,4,4,544]{3,2,1,0:T(4,128)S(1)} %copy.111, f32[3,4,144]{2,1,0:T(4,128)S(1)} %dynamic-slice_bitcast_fusion.5, f32[3,4,4,544]{3,2,1,0:T(4,128)S(1)} %copy.112), kind=kLoop, calls=%fused_computation.7.clone.1 | loop fusion | flops 16293888 | bytes 10242816 | tf_op jit(solution)/shard_map/while/body/eval_jaxpr/reduce_sum | solution.py:32
  324.3 6.3 %fusion.44 = (f32[4,4,144,544]{3,2,1,0:T(8,128)}, f32[4,4,144,544]{3,2,1,0:T(8,128)}) fusion(f32[4,4,144,544]{3,2,1,0:T(8,128)S(1)} %get-tuple-element.210), kind=kLoop, calls=%fused_computation.13.clone.1 | loop fusion | flops 5013504 | bytes 15040512 | tf_op jit(solution)/shard_map/while/body/eval_jaxpr/div | solution.py:33
  330.7 8.0 %fusion.45 = f32[3,4,144]{2,1,0:T(4,128)S(1)} fusion(f32[4,4,144,544]{3,2,1,0:T(8,128)S(1)} %copy-done.1, f32[3,4,4,544]{3,2,1,0:T(4,128)S(1)} %copy.112, f32[4,4,144,544]{3,2,1,0:T(8,128)} %get-tuple-element.211, f32[4,4,144,544]{3,2,1,0:T(8,128)} %get-tuple-element.212, f32[3,4,4,544]{3,2,1,0:T(4,128)S(1)} %copy.111, ...), kind=kLoop, calls=%fused_computation.11.clone.1 | loop fusion | flops 22559040 | bytes 15263232 | tf_op jit(solution)/shard_map/while/body/eval_jaxpr/reduce_sum | solution.py:40
  339.4 3.3 gather_fusion
  343.4 6.8 %fusion.43 = (f32[4,4,144,544]{3,2,1,0:T(8,128)S(1)}, f32[4,4,144,544]{3,2,1,0:T(8,128)}) fusion(f32[3,4,4,544]{3,2,1,0:T(4,128)S(1)} %copy.111, f32[3,4,144]{2,1,0:T(4,128)S(1)} %dynamic-slice_bitcast_fusion.5, f32[3,4,4,544]{3,2,1,0:T(4,128)S(1)} %copy.112), kind=kLoop, calls=%fused_computation.7.clone.1 | loop fusion | flops 16293888 | bytes 10242816 | tf_op jit(solution)/shard_map/while/body/eval_jaxpr/reduce_sum | solution.py:32
  350.2 6.3 %fusion.44 = (f32[4,4,144,544]{3,2,1,0:T(8,128)}, f32[4,4,144,544]{3,2,1,0:T(8,128)}) fusion(f32[4,4,144,544]{3,2,1,0:T(8,128)S(1)} %get-tuple-element.210), kind=kLoop, calls=%fused_computation.13.clone.1 | loop fusion | flops 5013504 | bytes 15040512 | tf_op jit(solution)/shard_map/while/body/eval_jaxpr/div | solution.py:33
  356.5 8.0 %fusion.45 = f32[3,4,144]{2,1,0:T(4,128)S(1)} fusion(f32[4,4,144,544]{3,2,1,0:T(8,128)S(1)} %copy-done.1, f32[3,4,4,544]{3,2,1,0:T(4,128)S(1)} %copy.112, f32[4,4,144,544]{3,2,1,0:T(8,128)} %get-tuple-element.211, f32[4,4,144,544]{3,2,1,0:T(8,128)} %get-tuple-element.212, f32[3,4,4,544]{3,2,1,0:T(4,128)S(1)} %copy.111, ...), kind=kLoop, calls=%fused_computation.11.clone.1 | loop fusion | flops 22559040 | bytes 15263232 | tf_op jit(solution)/shard_map/while/body/eval_jaxpr/reduce_sum | solution.py:40
  365.2 3.3 gather_fusion
  369.2 6.8 %fusion.43 = (f32[4,4,144,544]{3,2,1,0:T(8,128)S(1)}, f32[4,4,144,544]{3,2,1,0:T(8,128)}) fusion(f32[3,4,4,544]{3,2,1,0:T(4,128)S(1)} %copy.111, f32[3,4,144]{2,1,0:T(4,128)S(1)} %dynamic-slice_bitcast_fusion.5, f32[3,4,4,544]{3,2,1,0:T(4,128)S(1)} %copy.112), kind=kLoop, calls=%fused_computation.7.clone.1 | loop fusion | flops 16293888 | bytes 10242816 | tf_op jit(solution)/shard_map/while/body/eval_jaxpr/reduce_sum | solution.py:32
  376.0 6.3 %fusion.44 = (f32[4,4,144,544]{3,2,1,0:T(8,128)}, f32[4,4,144,544]{3,2,1,0:T(8,128)}) fusion(f32[4,4,144,544]{3,2,1,0:T(8,128)S(1)} %get-tuple-element.210), kind=kLoop, calls=%fused_computation.13.clone.1 | loop fusion | flops 5013504 | bytes 15040512 | tf_op jit(solution)/shard_map/while/body/eval_jaxpr/div | solution.py:33
  382.4 8.0 %fusion.45 = f32[3,4,144]{2,1,0:T(4,128)S(1)} fusion(f32[4,4,144,544]{3,2,1,0:T(8,128)S(1)} %copy-done.1, f32[3,4,4,544]{3,2,1,0:T(4,128)S(1)} %copy.112, f32[4,4,144,544]{3,2,1,0:T(8,128)} %get-tuple-element.211, f32[4,4,144,544]{3,2,1,0:T(8,128)} %get-tuple-element.212, f32[3,4,4,544]{3,2,1,0:T(4,128)S(1)} %copy.111, ...), kind=kLoop, calls=%fused_computation.11.clone.1 | loop fusion | flops 22559040 | bytes 15263232 | tf_op jit(solution)/shard_map/while/body/eval_jaxpr/reduce_sum | solution.py:40
  395.1 6.8 %fusion.43 = (f32[4,4,144,544]{3,2,1,0:T(8,128)S(1)}, f32[4,4,144,544]{3,2,1,0:T(8,128)}) fusion(f32[3,4,4,544]{3,2,1,0:T(4,128)S(1)} %copy.111, f32[3,4,144]{2,1,0:T(4,128)S(1)} %dynamic-slice_bitcast_fusion.5, f32[3,4,4,544]{3,2,1,0:T(4,128)S(1)} %copy.112), kind=kLoop, calls=%fused_computation.7.clone.1 | loop fusion | flops 16293888 | bytes 10242816 | tf_op jit(solution)/shard_map/while/body/eval_jaxpr/reduce_sum | solution.py:32
  401.8 6.3 %fusion.44 = (f32[4,4,144,544]{3,2,1,0:T(8,128)}, f32[4,4,144,544]{3,2,1,0:T(8,128)}) fusion(f32[4,4,144,544]{3,2,1,0:T(8,128)S(1)} %get-tuple-element.210), kind=kLoop, calls=%fused_computation.13.clone.1 | loop fusion | flops 5013504 | bytes 15040512 | tf_op jit(solution)/shard_map/while/body/eval_jaxpr/div | solution.py:33
  408.2 8.0 %fusion.45 = f32[3,4,144]{2,1,0:T(4,128)S(1)} fusion(f32[4,4,144,544]{3,2,1,0:T(8,128)S(1)} %copy-done.1, f32[3,4,4,544]{3,2,1,0:T(4,128)S(1)} %copy.112, f32[4,4,144,544]{3,2,1,0:T(8,128)} %get-tuple-element.211, f32[4,4,144,544]{3,2,1,0:T(8,128)} %get-tuple-element.212, f32[3,4,4,544]{3,2,1,0:T(4,128)S(1)} %copy.111, ...), kind=kLoop, calls=%fused_computation.11.clone.1 | loop fusion | flops 22559040 | bytes 15263232 | tf_op jit(solution)/shard_map/while/body/eval_jaxpr/reduce_sum | solution.py:40
  420.9 6.8 %fusion.43 = (f32[4,4,144,544]{3,2,1,0:T(8,128)S(1)}, f32[4,4,144,544]{3,2,1,0:T(8,128)}) fusion(f32[3,4,4,544]{3,2,1,0:T(4,128)S(1)} %copy.111, f32[3,4,144]{2,1,0:T(4,128)S(1)} %dynamic-slice_bitcast_fusion.5, f32[3,4,4,544]{3,2,1,0:T(4,128)S(1)} %copy.112), kind=kLoop, calls=%fused_computation.7.clone.1 | loop fusion | flops 16293888 | bytes 10242816 | tf_op jit(solution)/shard_map/while/body/eval_jaxpr/reduce_sum | solution.py:32
  427.7 6.3 %fusion.44 = (f32[4,4,144,544]{3,2,1,0:T(8,128)}, f32[4,4,144,544]{3,2,1,0:T(8,128)}) fusion(f32[4,4,144,544]{3,2,1,0:T(8,128)S(1)} %get-tuple-element.210), kind=kLoop, calls=%fused_computation.13.clone.1 | loop fusion | flops 5013504 | bytes 15040512 | tf_op jit(solution)/shard_map/while/body/eval_jaxpr/div | solution.py:33
  434.0 8.0 %fusion.45 = f32[3,4,144]{2,1,0:T(4,128)S(1)} fusion(f32[4,4,144,544]{3,2,1,0:T(8,128)S(1)} %copy-done.1, f32[3,4,4,544]{3,2,1,0:T(4,128)S(1)} %copy.112, f32[4,4,144,544]{3,2,1,0:T(8,128)} %get-tuple-element.211, f32[4,4,144,544]{3,2,1,0:T(8,128)} %get-tuple-element.212, f32[3,4,4,544]{3,2,1,0:T(4,128)S(1)} %copy.111, ...), kind=kLoop, calls=%fused_computation.11.clone.1 | loop fusion | flops 22559040 | bytes 15263232 | tf_op jit(solution)/shard_map/while/body/eval_jaxpr/reduce_sum | solution.py:40
  446.8 6.8 %fusion.43 = (f32[4,4,144,544]{3,2,1,0:T(8,128)S(1)}, f32[4,4,144,544]{3,2,1,0:T(8,128)}) fusion(f32[3,4,4,544]{3,2,1,0:T(4,128)S(1)} %copy.111, f32[3,4,144]{2,1,0:T(4,128)S(1)} %dynamic-slice_bitcast_fusion.5, f32[3,4,4,544]{3,2,1,0:T(4,128)S(1)} %copy.112), kind=kLoop, calls=%fused_computation.7.clone.1 | loop fusion | flops 16293888 | bytes 10242816 | tf_op jit(solution)/shard_map/while/body/eval_jaxpr/reduce_sum | solution.py:32
  453.5 6.3 %fusion.44 = (f32[4,4,144,544]{3,2,1,0:T(8,128)}, f32[4,4,144,544]{3,2,1,0:T(8,128)}) fusion(f32[4,4,144,544]{3,2,1,0:T(8,128)S(1)} %get-tuple-element.210), kind=kLoop, calls=%fused_computation.13.clone.1 | loop fusion | flops 5013504 | bytes 15040512 | tf_op jit(solution)/shard_map/while/body/eval_jaxpr/div | solution.py:33
  459.9 8.0 %fusion.45 = f32[3,4,144]{2,1,0:T(4,128)S(1)} fusion(f32[4,4,144,544]{3,2,1,0:T(8,128)S(1)} %copy-done.1, f32[3,4,4,544]{3,2,1,0:T(4,128)S(1)} %copy.112, f32[4,4,144,544]{3,2,1,0:T(8,128)} %get-tuple-element.211, f32[4,4,144,544]{3,2,1,0:T(8,128)} %get-tuple-element.212, f32[3,4,4,544]{3,2,1,0:T(4,128)S(1)} %copy.111, ...), kind=kLoop, calls=%fused_computation.11.clone.1 | loop fusion | flops 22559040 | bytes 15263232 | tf_op jit(solution)/shard_map/while/body/eval_jaxpr/reduce_sum | solution.py:40
  472.6 6.8 %fusion.43 = (f32[4,4,144,544]{3,2,1,0:T(8,128)S(1)}, f32[4,4,144,544]{3,2,1,0:T(8,128)}) fusion(f32[3,4,4,544]{3,2,1,0:T(4,128)S(1)} %copy.111, f32[3,4,144]{2,1,0:T(4,128)S(1)} %dynamic-slice_bitcast_fusion.5, f32[3,4,4,544]{3,2,1,0:T(4,128)S(1)} %copy.112), kind=kLoop, calls=%fused_computation.7.clone.1 | loop fusion | flops 16293888 | bytes 10242816 | tf_op jit(solution)/shard_map/while/body/eval_jaxpr/reduce_sum | solution.py:32
  479.4 6.3 %fusion.44 = (f32[4,4,144,544]{3,2,1,0:T(8,128)}, f32[4,4,144,544]{3,2,1,0:T(8,128)}) fusion(f32[4,4,144,544]{3,2,1,0:T(8,128)S(1)} %get-tuple-element.210), kind=kLoop, calls=%fused_computation.13.clone.1 | loop fusion | flops 5013504 | bytes 15040512 | tf_op jit(solution)/shard_map/while/body/eval_jaxpr/div | solution.py:33
  485.7 8.0 %fusion.45 = f32[3,4,144]{2,1,0:T(4,128)S(1)} fusion(f32[4,4,144,544]{3,2,1,0:T(8,128)S(1)} %copy-done.1, f32[3,4,4,544]{3,2,1,0:T(4,128)S(1)} %copy.112, f32[4,4,144,544]{3,2,1,0:T(8,128)} %get-tuple-element.211, f32[4,4,144,544]{3,2,1,0:T(8,128)} %get-tuple-element.212, f32[3,4,4,544]{3,2,1,0:T(4,128)S(1)} %copy.111, ...), kind=kLoop, calls=%fused_computation.11.clone.1 | loop fusion | flops 22559040 | bytes 15263232 | tf_op jit(solution)/shard_map/while/body/eval_jaxpr/reduce_sum | solution.py:40
  498.5 6.8 %fusion.43 = (f32[4,4,144,544]{3,2,1,0:T(8,128)S(1)}, f32[4,4,144,544]{3,2,1,0:T(8,128)}) fusion(f32[3,4,4,544]{3,2,1,0:T(4,128)S(1)} %copy.111, f32[3,4,144]{2,1,0:T(4,128)S(1)} %dynamic-slice_bitcast_fusion.5, f32[3,4,4,544]{3,2,1,0:T(4,128)S(1)} %copy.112), kind=kLoop, calls=%fused_computation.7.clone.1 | loop fusion | flops 16293888 | bytes 10242816 | tf_op jit(solution)/shard_map/while/body/eval_jaxpr/reduce_sum | solution.py:32
  505.2 6.3 %fusion.44 = (f32[4,4,144,544]{3,2,1,0:T(8,128)}, f32[4,4,144,544]{3,2,1,0:T(8,128)}) fusion(f32[4,4,144,544]{3,2,1,0:T(8,128)S(1)} %get-tuple-element.210), kind=kLoop, calls=%fused_computation.13.clone.1 | loop fusion | flops 5013504 | bytes 15040512 | tf_op jit(solution)/shard_map/while/body/eval_jaxpr/div | solution.py:33
  511.6 8.0 %fusion.45 = f32[3,4,144]{2,1,0:T(4,128)S(1)} fusion(f32[4,4,144,544]{3,2,1,0:T(8,128)S(1)} %copy-done.1, f32[3,4,4,544]{3,2,1,0:T(4,128)S(1)} %copy.112, f32[4,4,144,544]{3,2,1,0:T(8,128)} %get-tuple-element.211, f32[4,4,144,544]{3,2,1,0:T(8,128)} %get-tuple-element.212, f32[3,4,4,544]{3,2,1,0:T(4,128)S(1)} %copy.111, ...), kind=kLoop, calls=%fused_computation.11.clone.1 | loop fusion | flops 22559040 | bytes 15263232 | tf_op jit(solution)/shard_map/while/body/eval_jaxpr/reduce_sum | solution.py:40
  (253 shorter events, 59.5 us)
Async XLA Ops:
  6.5 514.7 %copy-start = (f32[144,144]{1,0:T(8,128)S(1)}, f32[144,144]{1,0:T(8,128)}, u32[]{:S(2)}) copy-start(f32[144,144]{1,0:T(8,128)} %param.17) | copy-start | bytes 248836
  6.5 25.9 %copy-start.4 = (s32[8,8]{1,0:T(8,128)S(1)}, s32[8,8]{1,0:T(8,128)}, u32[]{:S(2)}) copy-start(s32[8,8]{1,0:T(8,128)} %param.21) | copy-start | bytes 772
  6.5 26.1 %copy-start.5 = (s32[64,4]{0,1:T(4,128)S(1)}, s32[64,4]{0,1:T(4,128)}, u32[]{:S(2)}) copy-start(s32[64,4]{0,1:T(4,128)} %param.18) | copy-start | bytes 3076
  6.5 26.3 %copy-start.6 = (s32[64]{0:T(128)S(1)}, s32[64]{0:T(128)}, u32[]{:S(2)}) copy-start(s32[64]{0:T(128)} %param.19) | copy-start | bytes 772
  6.5 34.0 %reduce-scatter.2.cloned.1.call-start = ((), (), s32[]{:S(2)}) async-start(), calls=%async_computation.2 | async-start | bytes 327680 | tf_op jit(solution)/shard_map/reduce_scatter | solution.py:103
  8.7 21.6 %collective-permute-start = (f32[64,6,144]{2,0,1:T(8,128)S(1)}, f32[64,6,144]{2,0,1:T(8,128)S(1)}, u32[]{:S(2)}, u32[]{:S(2)}) collective-permute-start(f32[64,6,144]{2,0,1:T(8,128)S(1)} %pad_maximum_fusion.1), channel_id=1, source_target_pairs={{0,4},{4,8},{8,12},{12,16},{16,20},{20,24},{24,28},{1,5},{5,9},{9,... | collective-permute-start | bytes 663560 | tf_op jit(solution)/shard_map/ppermute | solution.py:22
  13.6 16.8 %collective-permute-start.1 = (f32[64,6,144]{2,0,1:T(8,128)S(1)}, f32[64,6,144]{2,0,1:T(8,128)S(1)}, u32[]{:S(2)}, u32[]{:S(2)}) collective-permute-start(f32[64,6,144]{2,0,1:T(8,128)S(1)} %pad_maximum_fusion.1), channel_id=1, source_target_pairs={{4,0},{8,4},{12,8},{16,12},{20,16},{24,20},{28,24},{5,1},{9,5},{13... | collective-permute-start | bytes 663560 | tf_op jit(solution)/shard_map/ppermute | solution.py:24
  17.9 88.8 %all-gather.2.cloned.1.call-start = ((), (), s32[]{:S(2)}) async-start(), calls=%async_computation.1 | async-start | bytes 7864320 | tf_op jit(solution)/shard_map/all_gather | solution.py:68
  30.4 76.3 %copy-start.2 = (f32[544,144]{0,1:T(8,128)S(1)}, f32[544,144]{0,1:T(8,128)}, u32[]{:S(2)}) copy-start(f32[544,144]{0,1:T(8,128)} %param.16) | copy-start | bytes 940036
  106.7 414.5 %copy-start.3 = (f32[64,3,144]{2,0,1:T(8,128)S(1)}, f32[64,3,144]{2,0,1:T(8,128)}, u32[]{:S(2)}) copy-start(f32[64,3,144]{2,0,1:T(8,128)} %param.14) | copy-start | bytes 331780
  117.6 6.4 %copy-start.1 = (f32[4,4,144,544]{3,2,1,0:T(8,128)S(1)}, f32[4,4,144,544]{3,2,1,0:T(8,128)}, u32[]{:S(2)}) copy-start(f32[4,4,144,544]{3,2,1,0:T(8,128)} %get-tuple-element.209) | copy-start | bytes 15040516 | tf_op jit(solution)/shard_map/while
  143.4 6.4 %copy-start.1 = (f32[4,4,144,544]{3,2,1,0:T(8,128)S(1)}, f32[4,4,144,544]{3,2,1,0:T(8,128)}, u32[]{:S(2)}) copy-start(f32[4,4,144,544]{3,2,1,0:T(8,128)} %get-tuple-element.209) | copy-start | bytes 15040516 | tf_op jit(solution)/shard_map/while
  169.3 6.4 %copy-start.1 = (f32[4,4,144,544]{3,2,1,0:T(8,128)S(1)}, f32[4,4,144,544]{3,2,1,0:T(8,128)}, u32[]{:S(2)}) copy-start(f32[4,4,144,544]{3,2,1,0:T(8,128)} %get-tuple-element.209) | copy-start | bytes 15040516 | tf_op jit(solution)/shard_map/while
  195.1 6.4 %copy-start.1 = (f32[4,4,144,544]{3,2,1,0:T(8,128)S(1)}, f32[4,4,144,544]{3,2,1,0:T(8,128)}, u32[]{:S(2)}) copy-start(f32[4,4,144,544]{3,2,1,0:T(8,128)} %get-tuple-element.209) | copy-start | bytes 15040516 | tf_op jit(solution)/shard_map/while
  220.9 6.4 %copy-start.1 = (f32[4,4,144,544]{3,2,1,0:T(8,128)S(1)}, f32[4,4,144,544]{3,2,1,0:T(8,128)}, u32[]{:S(2)}) copy-start(f32[4,4,144,544]{3,2,1,0:T(8,128)} %get-tuple-element.209) | copy-start | bytes 15040516 | tf_op jit(solution)/shard_map/while
  246.8 6.4 %copy-start.1 = (f32[4,4,144,544]{3,2,1,0:T(8,128)S(1)}, f32[4,4,144,544]{3,2,1,0:T(8,128)}, u32[]{:S(2)}) copy-start(f32[4,4,144,544]{3,2,1,0:T(8,128)} %get-tuple-element.209) | copy-start | bytes 15040516 | tf_op jit(solution)/shard_map/while
  272.6 6.4 %copy-start.1 = (f32[4,4,144,544]{3,2,1,0:T(8,128)S(1)}, f32[4,4,144,544]{3,2,1,0:T(8,128)}, u32[]{:S(2)}) copy-start(f32[4,4,144,544]{3,2,1,0:T(8,128)} %get-tuple-element.209) | copy-start | bytes 15040516 | tf_op jit(solution)/shard_map/while
  298.5 6.4 %copy-start.1 = (f32[4,4,144,544]{3,2,1,0:T(8,128)S(1)}, f32[4,4,144,544]{3,2,1,0:T(8,128)}, u32[]{:S(2)}) copy-start(f32[4,4,144,544]{3,2,1,0:T(8,128)} %get-tuple-element.209) | copy-start | bytes 15040516 | tf_op jit(solution)/shard_map/while
  324.3 6.4 %copy-start.1 = (f32[4,4,144,544]{3,2,1,0:T(8,128)S(1)}, f32[4,4,144,544]{3,2,1,0:T(8,128)}, u32[]{:S(2)}) copy-start(f32[4,4,144,544]{3,2,1,0:T(8,128)} %get-tuple-element.209) | copy-start | bytes 15040516 | tf_op jit(solution)/shard_map/while
  350.2 6.4 %copy-start.1 = (f32[4,4,144,544]{3,2,1,0:T(8,128)S(1)}, f32[4,4,144,544]{3,2,1,0:T(8,128)}, u32[]{:S(2)}) copy-start(f32[4,4,144,544]{3,2,1,0:T(8,128)} %get-tuple-element.209) | copy-start | bytes 15040516 | tf_op jit(solution)/shard_map/while
  376.0 6.4 %copy-start.1 = (f32[4,4,144,544]{3,2,1,0:T(8,128)S(1)}, f32[4,4,144,544]{3,2,1,0:T(8,128)}, u32[]{:S(2)}) copy-start(f32[4,4,144,544]{3,2,1,0:T(8,128)} %get-tuple-element.209) | copy-start | bytes 15040516 | tf_op jit(solution)/shard_map/while
  401.8 6.4 %copy-start.1 = (f32[4,4,144,544]{3,2,1,0:T(8,128)S(1)}, f32[4,4,144,544]{3,2,1,0:T(8,128)}, u32[]{:S(2)}) copy-start(f32[4,4,144,544]{3,2,1,0:T(8,128)} %get-tuple-element.209) | copy-start | bytes 15040516 | tf_op jit(solution)/shard_map/while
  427.7 6.4 %copy-start.1 = (f32[4,4,144,544]{3,2,1,0:T(8,128)S(1)}, f32[4,4,144,544]{3,2,1,0:T(8,128)}, u32[]{:S(2)}) copy-start(f32[4,4,144,544]{3,2,1,0:T(8,128)} %get-tuple-element.209) | copy-start | bytes 15040516 | tf_op jit(solution)/shard_map/while
  453.5 6.4 %copy-start.1 = (f32[4,4,144,544]{3,2,1,0:T(8,128)S(1)}, f32[4,4,144,544]{3,2,1,0:T(8,128)}, u32[]{:S(2)}) copy-start(f32[4,4,144,544]{3,2,1,0:T(8,128)} %get-tuple-element.209) | copy-start | bytes 15040516 | tf_op jit(solution)/shard_map/while
  479.4 6.4 %copy-start.1 = (f32[4,4,144,544]{3,2,1,0:T(8,128)S(1)}, f32[4,4,144,544]{3,2,1,0:T(8,128)}, u32[]{:S(2)}) copy-start(f32[4,4,144,544]{3,2,1,0:T(8,128)} %get-tuple-element.209) | copy-start | bytes 15040516 | tf_op jit(solution)/shard_map/while
  505.2 6.4 %copy-start.1 = (f32[4,4,144,544]{3,2,1,0:T(8,128)S(1)}, f32[4,4,144,544]{3,2,1,0:T(8,128)}, u32[]{:S(2)}) copy-start(f32[4,4,144,544]{3,2,1,0:T(8,128)} %get-tuple-element.209) | copy-start | bytes 15040516 | tf_op jit(solution)/shard_map/while
Sparse Core Ops, SparseCore 0:
  18.1 22.4 reduce-scatter.1
  42.2 64.4 all-gather.1
where the time goes:
time: 531 us; the launch traced here: 529 us
  other arithmetic  344 us (65%)
  local copies, waits for them, and re-layouts  75.4 us (14%)
  blocking collectives  59 us (11%)
  waiting for transfers between devices  21.6 us (4%)
  between operations  13.6 us (3%)
  matrix products  8.03 us (2%)
  starting transfers between devices  6.23 us (1%)
    reduce_sum x16, other arithmetic, near_block(): return jnp.sum(stokes(rel, sources[3:, :, :, None, :]), axis=2)  128 us
    reduce_sum x17, other arithmetic, stokes(): dist = jnp.sum(rel * rel, axis=0) + BLOB2  108 us
    div x17, other arithmetic, stokes(): inverse = 1.0 / (dist * jnp.sqrt(dist))  102 us
    gather x16, local copies, waits for them, and re-layouts, one_block(): chosen = pool[spots]  53.5 us
    all_gather x1, blocking collectives, shards(): everything = lax.all_gather(owned, ('domain', 'group'), axis=1, tiled=True)  51.2 us
    ppermute x1, waiting for transfers between devices, padded(): lax.ppermute(tail, axis, [(i, (i + 1) % count) for i in range(ends)])  12.4 us
  transfers between devices with their start and end apart: 4, of which 3 were waited for; matrix products, arithmetic and copies ran while one was open for 2% of the time, Pallas kernels for 0%

commit v1 on v0

v1 whole, which is shorter than its diff:
```python
import functools

import jax
import jax.numpy as jnp
from jax import lax
from jax.experimental import pallas as pl
from jax.experimental.pallas import tpu as pltpu
from jax.sharding import PartitionSpec as P

LEAF_CAP = 16
EPS = 0.5
UNITS = 4
BATCH = 32
PARTS = 6
F32 = jnp.float32
BF16 = jnp.bfloat16
HIGHEST = lax.Precision.HIGHEST
VMEM_SPEC = pl.BlockSpec(memory_space=pltpu.VMEM)
SMEM_SPEC = pl.BlockSpec(memory_space=pltpu.SMEM)


def params(mib):
    return pltpu.CompilerParams(vmem_limit_bytes=mib << 20)


def iota(shape, dim):
    return lax.broadcasted_iota(jnp.int32, shape, dim)


def split3(value):
    high = value.astype(BF16).astype(F32)
    rest = value - high
    mid = rest.astype(BF16).astype(F32)
    return high, mid, rest - mid


def stack_left(value, axis):
    h, m, l = split3(value)
    return jnp.concatenate([h, m, l, h, m, h], axis=axis)


def stack_right(value, axis):
    h, m, l = split3(value)
    return jnp.concatenate([h, h, h, m, m, l], axis=axis)


def dot_nt(a, b, precision=None):
    return lax.dot_general(
        a, b, (((1,), (1,)), ((), ())), precision=precision, preferred_element_type=F32
    )


def column(row):
    n = row.shape[1]
    eye = iota((n, n), 0) == iota((n, n), 1)
    return jnp.sum(jnp.where(eye, row, jnp.zeros_like(row)), axis=1, keepdims=True)


def as_row(col):
    n = col.shape[0]
    eye = iota((n, n), 0) == iota((n, n), 1)
    return jnp.sum(jnp.where(eye, col, jnp.zeros_like(col)), axis=0, keepdims=True)


def pack_kernel(cen_ref, off_ref, den_ref, area_ref, leaf_ref, list_ref, tile_ref, load_ref):
    rows, points = area_ref.shape
    area = area_ref[...]
    tail = points - 128
    tails = []
    lines = []
    for c in range(3):
        grid = off_ref[c] + column(cen_ref[c : c + 1, :])
        tile_ref[pl.ds(c, rows, 8), :] = grid[:, :128]
        tails.append(grid[:, 128:])
    for c in range(3):
        weighted = den_ref[c] * area
        tile_ref[pl.ds(3 + c, rows, 8), :] = weighted[:, :128]
        tails.append(weighted[:, 128:])
        lines.append(as_row(jnp.sum(weighted, axis=1, keepdims=True)))
    tails.append(jnp.zeros((rows, 128 - 6 * tail), F32))
    tile_ref[pl.ds(6, rows, 8), :] = jnp.concatenate(tails, axis=1)
    tile_ref[pl.ds(7, rows, 8), :] = jnp.zeros((rows, 128), F32)
    leaf = (leaf_ref[...] // LEAF_CAP).astype(F32)
    block = jnp.concatenate([cen_ref[...]] + lines + [leaf, jnp.zeros((1, rows), F32)], axis=0)
    lists = list_ref[...].astype(F32)
    rest = 128 - rows - lists.shape[1]
    load_ref[...] = jnp.concatenate([block, lists, jnp.zeros((8, rest), F32)], axis=1)


def pack(cen, off, den, area, leaf, lists):
    rows = area.shape[0]
    return pl.pallas_call(
        pack_kernel,
        out_shape=(
            jax.ShapeDtypeStruct((8 * rows, 128), F32),
            jax.ShapeDtypeStruct((8, 128), F32),
        ),
        in_specs=[VMEM_SPEC] * 6,
        out_specs=(VMEM_SPEC, VMEM_SPEC),
        compiler_params=params(32),
        name="pack",
    )(cen, off, den, area, leaf, lists)


def left_kernel(groups, place_ref, src_ref, cnt_ref, off_ref, den_ref, op_ref, up_ref,
                left_ref, self_ref, upw_ref, t1, s1, k1, t2, s2, k2, n_ref):
    _, rows, points = off_ref.shape
    slots = src_ref.shape[1]
    domain = place_ref[0]
    group = place_ref[1]

    def each_target(t, state):
        live = cnt_ref[t]
        a, b = state
        for k in range(slots):
            src = src_ref[t, k]
            step = src // (groups * rows) - domain
            turn = jnp.bitwise_xor(src // rows % groups, group)
            near = step == 0
            base = turn * rows + src % rows
            is_live = k < live
            t1[a] = t
            s1[a] = base
            k1[a] = k
            t2[b] = t
            s2[b] = base + jnp.where(step > 0, groups * rows, 0)
            k2[b] = k
            a += jnp.where(jnp.logical_and(is_live, near), 1, 0)
            b += jnp.where(jnp.logical_and(is_live, jnp.logical_not(near)), 1, 0)
        return a, b

    a, b = lax.fori_loop(0, rows, each_target, (0, 0))
    n_ref[0] = a
    n_ref[1] = b

    def pad_one(i, _):
        t1[a + i] = 0
        k1[a + i] = 0
        s1[a + i] = groups * rows
        t2[b + i] = 0
        k2[b + i] = 0
        s2[b + i] = 2 * groups * rows
        return 0

    lax.fori_loop(0, BATCH + 2 * UNITS, pad_one, 0)

    eye = (iota((points, points), 0) == iota((points, points), 1)).astype(BF16)

    def one_left(t, _):
        x = [off_ref[c, pl.ds(t, 1), :] * (1.0 / EPS) for c in range(3)]
        xx = x[0] * x[0] + x[1] * x[1] + x[2] * x[2]
        one = jnp.ones_like(xx)
        zero = jnp.zeros_like(xx)
        cases = [[xx]]
        for c in range(3):
            cases.append([xx + x[c] * x[c], x[c] * x[(c + 1) % 3], x[c] * x[(c + 2) % 3]])
        for o, extra in enumerate(cases):
            lines = x + [one] + extra
            lines += [zero] * (8 - len(lines))
            stacked = stack_left(jnp.concatenate(lines, axis=0), 0).astype(BF16)
            left_ref[t, o, :, : 8 * PARTS] = dot_nt(eye, stacked).astype(BF16)
        return 0

    lax.fori_loop(0, rows, one_left, 0)

    for c in range(3):
        self_ref[c] = dot_nt(den_ref[c], op_ref[...], HIGHEST)

    fine = up_ref.shape[1]
    full = fine // 128 * 128
    rest = fine - full
    tail = points - 128
    up = up_ref[...]
    wide = jnp.concatenate([up[:, :full]] + [up[:, full:]] * (128 // rest), axis=1)
    weights = jnp.concatenate(
        [wide[:128]] + [wide[128:]] * 6 + [jnp.zeros((128 - 6 * tail, full + 128), F32)], axis=0
    )
    for i, part in enumerate(split3(weights)):
        upw_ref[i] = part.astype(BF16)


def left(groups, place, src, cnt, off, den, op, up_t):
    rows, slots = src.shape
    points = off.shape[2]
    fine = up_t.shape[1]
    size = rows * slots + BATCH + 2 * UNITS
    ints = jax.ShapeDtypeStruct((size,), jnp.int32)
    return pl.pallas_call(
        functools.partial(left_kernel, groups),
        out_shape=(
            jax.ShapeDtypeStruct((rows, 4, points, 128), BF16),
            jax.ShapeDtypeStruct((3, rows, points), F32),
            jax.ShapeDtypeStruct((3, 256, fine // 128 * 128 + 128), BF16),
        )
        + (ints,) * 6
        + (jax.ShapeDtypeStruct((2,), jnp.int32),),
        in_specs=[SMEM_SPEC] * 3 + [VMEM_SPEC] * 4,
        out_specs=(VMEM_SPEC,) * 3 + (SMEM_SPEC,) * 7,
        compiler_params=params(40),
        name="left",
    )(place, src, cnt, off, den, op, up_t)


def right(tile):
    width = tile.shape[1]
    sub = iota((8, width), 0)
    y = [tile[c : c + 1] for c in range(3)]
    f = [tile[3 + c : 4 + c] for c in range(3)]
    yy = y[0] * y[0] + y[1] * y[1] + y[2] * y[2]
    yf = y[0] * f[0] + y[1] * f[1] + y[2] * f[2]
    zero = jnp.zeros_like(yy)
    one = jnp.ones_like(yy)
    points = jnp.concatenate([y[0], y[1], y[2], -0.5 * yy - 1.0] + [zero] * 4, axis=0)
    forces = jnp.concatenate([f[0], f[1], f[2], -yf] + [zero] * 4, axis=0)
    outs = [
        jnp.concatenate(
            [-2.0 * y[0], -2.0 * y[1], -2.0 * y[2], yy + 1.0, one] + [zero] * 3, axis=0
        )
    ]
    for c in range(3):
        extra = jnp.concatenate([zero] * 4 + [f[c], f[(c + 1) % 3], f[(c + 2) % 3], zero], axis=0)
        extra = jnp.where(sub == c, -yf, extra)
        outs.append(extra - 2.0 * f[c] * points - y[c] * forces)
    return [stack_right(v, 0).astype(BF16) for v in outs]


def shifted(tile, center):
    sub = iota(tile.shape, 0)
    shift = jnp.where(sub == 0, center[0], jnp.where(sub == 1, center[1], center[2]))
    return jnp.where(sub < 3, (tile - shift) * (1.0 / EPS), tile)


def evaluate(lefts, rights, width):
    sums = [0.0, 0.0, 0.0]
    total = rights[0].shape[1]
    for start in range(0, total, width):
        cut = slice(start, start + width)
        dist, *tops = [
            jnp.dot(lefts[o], rights[o][:, cut], preferred_element_type=F32) for o in range(4)
        ]
        u = lax.rsqrt(dist)
        w = u * u * u
        for c in range(3):
            product = w * tops[c]
            for j in range(0, width, 128):
                sums[c] = sums[c] + product[:, j : j + 128]
    return [jnp.sum(s, axis=1, keepdims=True) for s in sums]


def near_kernel(n_blocks, which, last, *refs):
    t_ref, s_ref, k_ref, n_ref, cen_ref = refs[:5]
    refs = refs[5:]
    blocks = refs[:n_blocks]
    left_ref, upw_ref = refs[n_blocks : n_blocks + 2]
    refs = refs[n_blocks + 2 :]
    if last:
        cols_in, tail_in, self_ref, far_ref = refs[:4]
        out_ref = refs[4]
        refs = refs[5:]
    else:
        cols_out, tail_out = refs[:2]
        refs = refs[2:]
    if last:
        pool, fine, tails, cols, rows_a, rows_b, wa, wb = refs
    else:
        pool, fine, rows_a, rows_b, wa, wb = refs
        cols, tails = cols_out, tail_out

    rows = left_ref.shape[0]
    points = left_ref.shape[2]
    full = upw_ref.shape[2] - 128
    held = blocks[0].shape[0]
    for i, block in enumerate(blocks):
        pool[pl.ds(i * held, held)] = block[...]
    pool[n_blocks * held] = jnp.zeros((8, 128), F32)
    if last:
        cols[...] = cols_in[...]
        tails[...] = tail_in[...]
    else:
        cols[...] = jnp.zeros_like(cols)
        tails[...] = jnp.zeros_like(tails)

    n = n_ref[which]
    sub = iota((8, 128), 0)
    lane = iota((8, 128), 1)
    own_lanes = lane // (points - 128) == sub
    k_lane = lane // 32

    def upsample(b, _):
        for j in range(BATCH):
            tile = pool[s_ref[b * BATCH + j]]
            rows_a[pl.ds(8 * j, 8), :] = jnp.where(sub < 6, tile, 0.0)
            rows_b[pl.ds(8 * j, 8), :] = jnp.where(
                jnp.logical_and(own_lanes, sub < 6), tile[6:7, :], 0.0
            )
        value = jnp.concatenate([rows_a[...], rows_b[...]], axis=1)
        h, m, l = [v.astype(BF16) for v in split3(value)]
        uh, um, ul = upw_ref[0], upw_ref[1], upw_ref[2]
        out = None
        for a, w in ((h, uh), (h, um), (m, uh), (h, ul), (l, uh), (m, um)):
            term = jnp.dot(a, w, preferred_element_type=F32)
            out = term if out is None else out + term
        out = out.reshape(BATCH, 8, full + 128)
        fine[pl.ds(b * BATCH, BATCH)] = out[:, :, :full]
        for j in range(BATCH):
            i = b * BATCH + j
            t = t_ref[i]
            mine = jnp.logical_and(k_lane == k_ref[i], i < n)
            tails[t] = jnp.where(mine, out[j, :, full:], tails[t])
        return 0

    lax.fori_loop(0, (n + BATCH - 1) // BATCH, upsample, 0)

    lane_p = iota((points, 128), 1)

    def add_cols(t, sums):
        for c in range(3):
            cols[c] += jnp.where(lane_p == t, sums[c], 0.0)

    def center_of(t):
        return [cen_ref[c, t] for c in range(3)]

    def build(i, w):
        for j in range(UNITS):
            u = i * UNITS + j
            for o, v in enumerate(right(shifted(fine[u], center_of(t_ref[u])))):
                w[j, o] = v

    def main(i, w):
        found = []
        for j in range(UNITS):
            t = t_ref[i * UNITS + j]
            lefts = [left_ref[t, o, :, : 8 * PARTS] for o in range(4)]
            rights = [w[j, o] for o in range(4)]
            found.append((t, evaluate(lefts, rights, 256)))
        for c in range(3):
            value = cols[c]
            for t, sums in found:
                value = value + jnp.where(lane_p == t, sums[c], 0.0)
            cols[c] = value

    build(0, wa)

    def two(i, _):
        build(2 * i + 1, wb)
        main(2 * i, wa)
        build(2 * i + 2, wa)
        main(2 * i + 1, wb)
        return 0

    lax.fori_loop(0, (n + 2 * UNITS - 1) // (2 * UNITS), two, 0)

    if last:
        each = 4

        def tail_pass(i, _):
            found = []
            for j in range(each):
                t = i * each + j
                lefts = [left_ref[t, o, :, : 8 * PARTS] for o in range(4)]
                found.append((t, evaluate(lefts, right(shifted(tails[t], center_of(t))), 128)))
            for c in range(3):
                value = cols[c]
                for t, sums in found:
                    value = value + jnp.where(lane_p == t, sums[c], 0.0)
                cols[c] = value
            return 0

        lax.fori_loop(0, rows // each, tail_pass, 0)
        for c in range(3):
            turned = jnp.transpose(cols[c])[:rows]
            out_ref[c] = turned * (1.0 / EPS) + self_ref[c] + far_ref[c][:, :1]


def near(which, last, blocks, lists, counts, cen, lefts, upw, extra):
    t, s, k = lists
    rows, _, points, _ = lefts.shape
    full = upw.shape[2] - 128
    held = blocks[0].shape[0]
    n_blocks = len(blocks)
    size = t.shape[0]
    cols = jax.ShapeDtypeStruct((3, points, 128), F32)
    tails = jax.ShapeDtypeStruct((rows, 8, 128), F32)
    if last:
        out_shape = jax.ShapeDtypeStruct((3, rows, points), F32)
        out_specs = VMEM_SPEC
    else:
        out_shape = (cols, tails)
        out_specs = (VMEM_SPEC, VMEM_SPEC)
    scratch = [
        pltpu.VMEM((n_blocks * held + 1, 8, 128), F32),
        pltpu.VMEM((size, 8, full), F32),
    ]
    if last:
        scratch += [pltpu.VMEM(tails.shape, F32), pltpu.VMEM(cols.shape, F32)]
    scratch += [pltpu.VMEM((8 * BATCH, 128), F32)] * 2
    scratch += [pltpu.VMEM((UNITS, 4, 8 * PARTS, full), BF16)] * 2
    return pl.pallas_call(
        functools.partial(near_kernel, n_blocks, which, last),
        out_shape=out_shape,
        in_specs=[SMEM_SPEC] * 5 + [VMEM_SPEC] * (n_blocks + 2 + len(extra)),
        out_specs=out_specs,
        scratch_shapes=scratch,
        compiler_params=params(56),
        name="near_last" if last else "near_own",
    )(t, s, k, counts, cen, *blocks, lefts, upw, *extra)


def far_kernel(groups, place_ref, mine_ref, all_ref, far_ref):
    rows = far_ref.shape[1]
    devices = all_ref.shape[0]
    domain = place_ref[0]
    mine = mine_ref[...]
    block = mine[:, :rows]
    center = [column(block[c : c + 1]) for c in range(3)]
    leaf = column(block[6:7])
    leaves = jnp.concatenate(
        [all_ref[domain * groups + g][:, rows : rows + 8] for g in range(groups)], axis=0
    )
    count = groups * 8
    first = (domain * count).astype(F32)
    hot = (leaf - first == iota((rows, count), 1).astype(F32)).astype(F32)
    lists = jnp.dot(hot, leaves, precision=HIGHEST, preferred_element_type=F32)
    lists = jnp.round(lists)
    wanted = [lists[:, k : k + 1] for k in range(8)]
    lane = iota((8, 128), 1)

    def one(i, sums):
        both = jnp.where(lane < 64, all_ref[2 * i], pltpu.roll(all_ref[2 * i + 1], 64, 1))
        rel = [center[c] - both[c : c + 1] for c in range(3)]
        force = [both[3 + c : 4 + c] for c in range(3)]
        source = both[6:7]
        times = jnp.zeros((rows, 128), F32)
        for k in range(8):
            times = times + jnp.where(wanted[k] == source, 1.0, 0.0)
        dist = rel[0] * rel[0] + rel[1] * rel[1] + rel[2] * rel[2] + EPS * EPS
        u = lax.rsqrt(dist)
        u3 = u * u * u * times
        near_part = (dist + EPS * EPS) * u3
        project = (rel[0] * force[0] + rel[1] * force[1] + rel[2] * force[2]) * u3
        return [sums[c] + near_part * force[c] + project * rel[c] for c in range(3)]

    sums = lax.fori_loop(0, devices // 2, one, [jnp.zeros((rows, 128), F32)] * 3)
    for c in range(3):
        far_ref[c] = jnp.broadcast_to(jnp.sum(sums[c], axis=1, keepdims=True), (rows, 128))


def far_field(groups, place, mine, everything, rows):
    return pl.pallas_call(
        functools.partial(far_kernel, groups),
        out_shape=jax.ShapeDtypeStruct((3, rows, 128), F32),
        in_specs=[SMEM_SPEC, VMEM_SPEC, VMEM_SPEC],
        out_specs=VMEM_SPEC,
        compiler_params=params(32),
        name="far",
    )(place, mine, everything)


def swap(x, axis, bit):
    return lax.ppermute(x, axis, [(i, i ^ bit) for i in range(lax.axis_size(axis))])


def bits(n):
    found = []
    bit = 1
    while bit < n:
        found.append(bit)
        bit *= 2
    return found


def shards(
    centers,
    offsets,
    density,
    area,
    upsample,
    self_operator,
    near_sources,
    near_counts,
    leaf_slot,
    leaf_list,
):
    rows = centers.shape[0]
    groups = lax.axis_size("group")
    domains = lax.axis_size("domain")
    place = jnp.stack([lax.axis_index("domain"), lax.axis_index("group")]).astype(jnp.int32)
    cen = centers.T
    off = jnp.transpose(offsets, (1, 0, 2))
    den = jnp.transpose(density, (1, 0, 2))
    tiles, load = pack(cen, off, den, area, leaf_slot[None, :], leaf_list)
    tiles = tiles.reshape(rows, 8, 128)
    ends = domains - 1
    above = lax.ppermute(tiles, "domain", [(i + 1, i) for i in range(ends)])
    below = lax.ppermute(tiles, "domain", [(i, i + 1) for i in range(ends)])
    own = [tiles]
    sides = [[below], [above]]
    for bit in reversed(bits(groups)):
        own = own + [swap(v, "group", bit) for v in own]
        sides = [side + [swap(v, "group", bit) for v in side] for side in sides]
    order = [0]
    for bit in reversed(bits(groups)):
        order = order + [i ^ bit for i in order]
    rank = [order.index(i) for i in range(groups)]
    own = [own[i] for i in rank]
    sides = [[side[i] for i in rank] for side in sides]

    everything = load[None]
    for axis, size in (("domain", domains), ("group", groups)):
        for bit in reversed(bits(size)):
            everything = jnp.concatenate([everything, swap(everything, axis, bit)], axis=0)
    spots = [0]
    for bit in reversed(bits(domains)):
        spots = spots + [i ^ bit for i in spots]
    spots = [i * groups for i in spots]
    for bit in reversed(bits(groups)):
        spots = spots + [i ^ bit for i in spots]

    lefts, self_term, upw, t1, s1, k1, t2, s2, k2, counts = left(
        groups, place, near_sources, near_counts, off, den, self_operator, upsample.T
    )
    far = far_field(groups, place, load, sort_loads(everything, spots, place, groups), rows)
    cols, tails = near(0, False, own, (t1, s1, k1), counts, cen, lefts, upw, ())
    out = near(
        1,
        True,
        sides[0] + sides[1],
        (t2, s2, k2),
        counts,
        cen,
        lefts,
        upw,
        (cols, tails, self_term, far),
    )
    return jnp.transpose(out, (1, 0, 2))


def sort_loads(held, spots, place, groups):
    position = [0] * len(spots)
    for i, spot in enumerate(spots):
        position[spot] = i
    table = jnp.asarray(position, jnp.int32)
    me = place[0] * groups + place[1]
    return held[table[jnp.arange(len(spots), dtype=jnp.int32) ^ me]]


def solution(mesh):
    in_specs = (
        P(("domain", "group"), None),
        P(("domain", "group"), None, None),
        P(("domain", "group"), None, None),
        P(("domain", "group"), None),
        P(),
        P(),
        P(("domain", "group"), None),
        P(("domain", "group")),
        P(("domain", "group")),
        P(("domain", "group"), None),
    )
    out_specs = P(("domain", "group"), None, None)
    return jax.shard_map(shards, mesh=mesh, in_specs=in_specs, out_specs=out_specs, check_vma=False)
```

time: 531 us -> 145 us (0.27)
  other arithmetic: 344 us -> 0.11 us
  Pallas kernels: 0 us -> 85.2 us
  blocking collectives: 59 us -> 0 us
  local copies, waits for them, and re-layouts: 75.4 us -> 22.3 us
  between operations: 13.6 us -> 0.24 us
  starting transfers between devices: 6.23 us -> 17.3 us
  matrix products: 8.03 us -> 0 us
    reduce_sum x35 -> x0, other arithmetic: 238 us -> none  [the longest x16 128 us: near_block(): return jnp.sum(stokes(rel, sources[3:, :, :, None, :]), axis=2)]
    div x17 -> x0, other arithmetic: 102 us -> none  [stokes(): inverse = 1.0 / (dist * jnp.sqrt(dist))]
    pallas_call x0 -> x5, Pallas kernels: none -> 85.2 us  [the longest x2 58.6 us: near(): pl.pallas_call(functools.partial(near_kernel, n_blocks, which, last), out...]
    all_gather x2 -> x0, blocking collectives: 59 us -> none  [the longest x1 51.2 us: shards(): everything = lax.all_gather(owned, ('domain', 'group'), axis=1, tiled=True)]
    gather x19 -> x2, local copies, waits for them, and re-layouts: 56.9 us -> 1.94 us  [sort_loads(): return held[table[jnp.arange(len(spots), dtype=jnp.int32) ^ me]]]
    unnamed x14 -> x73, local copies, waits for them, and re-layouts: 0.89 us -> 20.4 us
    ppermute x2 -> x16, starting transfers between devices: 6.16 us -> 17.3 us  [the longest x14 12.6 us: swap(): lax.ppermute(x, axis, [(i, i ^ bit) for i in range(lax.axis_size(axis))])]
    dynamic_update_slice x16 -> x0, local copies, waits for them, and re-layouts: 9.72 us -> none  [shards(): lax.map(one_block, (grid.reshape(turns, block, 3, points), position.resha...]
  transfers between devices with their start and end apart: 4 -> 16, of which waited for: 3 -> 7; matrix products, arithmetic and copies ran while one was open for 2% -> 2% of each run, Pallas kernels for 0% -> 39%
where the time goes in v1:
time: 145 us; the launch traced here: 144 us
  Pallas kernels  85.2 us (59%)
  local copies, waits for them, and re-layouts  22.3 us (15%)
  waiting for transfers between devices  18.9 us (13%)
  starting transfers between devices  17.3 us (12%)
    pallas_call x2, Pallas kernels, near(): pl.pallas_call(functools.partial(near_kernel, n_blocks, which, last), out...  58.6 us
    pallas_call x1, Pallas kernels, left(): pl.pallas_call(functools.partial(left_kernel, groups), out_shape=(jax.Sha...  22.9 us
    unnamed x73, local copies, waits for them, and re-layouts  20.4 us
    ppermute x14, waiting for transfers between devices, swap(): lax.ppermute(x, axis, [(i, i ^ bit) for i in range(lax.axis_size(axis))])  18.9 us
    ppermute x14, starting transfers between devices, swap(): lax.ppermute(x, axis, [(i, i ^ bit) for i in range(lax.axis_size(axis))])  12.6 us
    pallas_call x1, Pallas kernels, far_field(): pl.pallas_call(functools.partial(far_kernel, groups), out_shape=jax.Shape...  3.45 us
    ppermute x1, starting transfers between devices, shards(): below = lax.ppermute(tiles, 'domain', [(i, i + 1) for i in range(ends)])  3.4 us
  transfers between devices with their start and end apart: 16, of which 7 were waited for; matrix products, arithmetic and copies ran while one was open for 2% of the time, Pallas kernels for 39%

profile of v1, /device:TPU:0, one launch (start us, length us, event | category | flops | bytes accessed | tf_op | source)
XLA Modules:
  0.0 144.1 jit_solution(6864824626414272069)
XLA Ops:
  0.0 0.9 copy-done.2
  0.9 0.9 copy-done.4
  1.9 0.8 copy-done.11
  2.7 0.7 copy-done.12
  3.4 0.7 copy-done.13
  4.1 0.7 copy-done.22
  4.7 0.2 pack.1
  4.9 3.0 %collective-permute-start.9 = (f32[64,8,128]{2,1,0:T(8,128)S(1)}, f32[64,8,128]{2,1,0:T(8,128)S(1)}, u32[]{:S(2)}, u32[]{:S(2)}) collective-permute-start(f32[64,8,128]{2,1,0:T(8,128)S(1)} %bitcast.23), channel_id=1, source_target_pairs={{0,2},{1,3},{2,0},{3,1},{4,6},{5,7},{6,4},{7,5},{8,10},{9,11},{10,... | collective-permute-start | bytes 786440 | tf_op jit(solution)/shard_map/ppermute | solution.py:460
  8.0 0.0 collective-permute-start.8
  8.0 3.4 %collective-permute-start = (f32[64,8,128]{2,1,0:T(8,128)S(1)}, f32[64,8,128]{2,1,0:T(8,128)S(1)}, u32[]{:S(2)}, u32[]{:S(2)}) collective-permute-start(f32[64,8,128]{2,1,0:T(8,128)S(1)} %bitcast.25), channel_id=1, source_target_pairs={{0,4},{4,8},{8,12},{12,16},{16,20},{20,24},{24,28},{1,5},{5,9},{9,... | collective-permute-start | bytes 786440 | tf_op jit(solution)/shard_map/ppermute | solution.py:495
  11.4 1.3 collective-permute-start.4
  12.7 4.7 %collective-permute-start.11 = (f32[1,8,128]{2,1,0:T(8,128)S(1)}, f32[1,8,128]{2,1,0:T(8,128)S(1)}, u32[]{:S(2)}, u32[]{:S(2)}) collective-permute-start(f32[1,8,128]{2,1,0:T(8,128)S(1)} %bitcast.28), channel_id=1, source_target_pairs={{0,16},{4,20},{8,24},{12,28},{16,0},{20,4},{24,8},{28,12},{1,17},{... | collective-permute-start | bytes 12296 | tf_op jit(solution)/shard_map/ppermute | solution.py:460
  17.4 1.4 gather_fusion
  18.7 5.1 %collective-permute-done.11 = f32[1,8,128]{2,1,0:T(8,128)S(1)} collective-permute-done((f32[1,8,128]{2,1,0:T(8,128)S(1)}, f32[1,8,128]{2,1,0:T(8,128)S(1)}, u32[]{:S(2)}, u32[]{:S(2)}) %collective-permute-start.11) | collective-permute-done | bytes 4128 | tf_op jit(solution)/shard_map/ppermute | solution.py:460
  23.8 1.6 %collective-permute-start.12 = (f32[2,8,128]{2,1,0:T(8,128)S(1)}, f32[2,8,128]{2,1,0:T(8,128)S(1)}, u32[]{:S(2)}, u32[]{:S(2)}) collective-permute-start(f32[2,8,128]{2,1,0:T(8,128)S(1)} %pad_maximum_fusion.2), channel_id=1, source_target_pairs={{0,8},{4,12},{8,0},{12,4},{16,24},{20,28},{24,16},{28,20},{1,9},{5... | collective-permute-start | bytes 24584 | tf_op jit(solution)/shard_map/ppermute | solution.py:460
  25.4 2.1 %collective-permute-done.12 = f32[2,8,128]{2,1,0:T(8,128)S(1)} collective-permute-done((f32[2,8,128]{2,1,0:T(8,128)S(1)}, f32[2,8,128]{2,1,0:T(8,128)S(1)}, u32[]{:S(2)}, u32[]{:S(2)}) %collective-permute-start.12) | collective-permute-done | bytes 8224 | tf_op jit(solution)/shard_map/ppermute | solution.py:460
  27.5 0.0 collective-permute-start.13
  27.5 3.7 %collective-permute-done.13 = f32[4,8,128]{2,1,0:T(8,128)S(1)} collective-permute-done((f32[4,8,128]{2,1,0:T(8,128)S(1)}, f32[4,8,128]{2,1,0:T(8,128)S(1)}, u32[]{:S(2)}, u32[]{:S(2)}) %collective-permute-start.13) | collective-permute-done | bytes 16416 | tf_op jit(solution)/shard_map/ppermute | solution.py:460
  31.2 0.5 collective-permute-start.14
  31.7 0.0 collective-permute-done.refs_5_
  31.8 1.6 %collective-permute-start.2 = (f32[64,8,128]{2,1,0:T(8,128)S(1)}, f32[64,8,128]{2,1,0:T(8,128)S(1)}, u32[]{:S(2)}, u32[]{:S(2)}) collective-permute-start(f32[64,8,128]{2,1,0:T(8,128)S(1)} %collective-permute-done.refs_5_), channel_id=1, source_target_pairs={{0,2},{1,3},{2,0},{3,1},{4,6},{5,7},{6,4},{7,5},{8,10},{9,11},{10,... | collective-permute-start | bytes 786440 | tf_op jit(solution)/shard_map/ppermute | solution.py:460
  33.3 0.0 collective-permute-done.4.refs_9_
  33.3 0.5 collective-permute-start.6
  33.9 1.7 %collective-permute-done.14 = f32[8,8,128]{2,1,0:T(8,128)S(1)} collective-permute-done((f32[8,8,128]{2,1,0:T(8,128)S(1)}, f32[8,8,128]{2,1,0:T(8,128)S(1)}, u32[]{:S(2)}, u32[]{:S(2)}) %collective-permute-start.14) | collective-permute-done | bytes 32800 | tf_op jit(solution)/shard_map/ppermute | solution.py:460
  35.6 0.0 collective-permute-start.15
  35.6 1.2 collective-permute-done.15
  36.8 0.2 collective-permute-start.1
  37.0 0.0 collective-permute-done.9.refs_7_
  37.0 0.4 collective-permute-start.5
  37.3 0.0 collective-permute-done.8.refs_6_
  37.3 0.2 collective-permute-start.10
  37.5 2.3 %collective-permute-done.2.refs_7_ = f32[64,8,128]{2,1,0:T(8,128)S(1)} collective-permute-done((f32[64,8,128]{2,1,0:T(8,128)S(1)}, f32[64,8,128]{2,1,0:T(8,128)S(1)}, u32[]{:S(2)}, u32[]{:S(2)}) %collective-permute-start.2) | collective-permute-done | bytes 262176 | tf_op jit(solution)/shard_map/ppermute | solution.py:460
  39.8 2.8 %collective-permute-done.6.refs_11_ = f32[64,8,128]{2,1,0:T(8,128)S(1)} collective-permute-done((f32[64,8,128]{2,1,0:T(8,128)S(1)}, f32[64,8,128]{2,1,0:T(8,128)S(1)}, u32[]{:S(2)}, u32[]{:S(2)}) %collective-permute-start.6) | collective-permute-done | bytes 262176 | tf_op jit(solution)/shard_map/ppermute | solution.py:460
  42.6 0.0 collective-permute-start.7
  42.6 0.1 pad_add_fusion.place_ref
  42.7 0.8 copy.13.src_ref
  43.5 0.9 copy-done.3
  44.4 0.9 copy-done.5
  45.3 1.0 copy-done.7
  46.3 0.9 copy-done.10
  47.2 0.7 copy-done.21
  47.9 22.9 %left.1 = (bf16[64,4,144,128]{3,2,1,0:T(8,128)(2,1)S(1)}, f32[3,64,144]{2,1,0:T(8,128)S(1)}, bf16[3,256,640]{2,1,0:T(8,128)(2,1)S(1)}, s32[296]{0:T(512)S(1)}, s...) custom-call(s32[2]{0:T(128)S(1)} %pad_add_fusion.place_ref, ...), custom_call_target="tpu_custom_call" | custom-call | tf_op jit(solution)/shard_map/left/pallas_call | solution.py:188
  70.8 3.6 %copy-done = bf16[64,4,144,128]{3,2,1,0:T(8,128)(2,1)} copy-done((bf16[64,4,144,128]{3,2,1,0:T(8,128)(2,1)}, bf16[64,4,144,128]{3,2,1,0:T(8,128)(2,1)S(1)}, u32[]{:S(2)}) %copy-start) | copy-done | bytes 9437208
  74.4 0.9 copy-done.1
  75.4 0.7 copy-done.9
  76.1 0.6 copy-done.17
  76.7 0.6 copy-done.18
  77.2 0.6 copy-done.19
  77.8 0.6 copy-done.20
  78.4 0.6 copy-done.14
  79.0 0.0 copy-done.15
  79.0 0.6 gather_fusion.1
  79.6 3.5 %far.1.refs_18_ = f32[3,64,128]{2,1,0:T(8,128)S(1)} custom-call(s32[2]{0:T(128)S(1)} %pad_add_fusion.place_ref, f32[8,128]{1,0:T(8,128)S(1)} %get-tuple-element.32.mine_ref, f32[32,8,128]{2,1,0:T(8,128)S(1)} %gather_fusion.1), custom_call_target="tpu_custom_call" | custom-call | tf_op jit(solution)/shard_map/far/pallas_call | solution.py:449
  83.1 0.6 copy-done.6
  83.7 0.0 collective-permute-done.10.refs_8_
  83.7 0.7 copy-done.25
  84.4 30.1 %near_own.1 = (f32[3,144,128]{2,1,0:T(8,128)}, f32[64,8,128]{2,1,0:T(8,128)}) custom-call(s32[296]{0:T(512)} %copy-done.14, s32[296]{0:T(512)} %copy-done.15, s32[296]{0:T(512)} %copy-done.16, s32[2]{0:T(128)} %copy-done.20, f32[3,64]{1,0:T(4,128)} %bitcast.32, f32[64,8,128]{2,1,0:T(8,128)} %bitcast.27, f32[64,8,128]{2,1,0:T(8,128)} %copy-done.24, ...), custom_call_target="tpu_custom_call" | custom-call | tf_op jit(solution)/shard_map/near_own/pallas_call | solution.py:398
  114.5 0.0 collective-permute-done.3.refs_8_
  114.6 0.0 collective-permute-done.7.refs_12_
  114.6 0.6 copy-done.30
  115.2 0.1 copy-done.31
  115.3 0.1 copy-done.32
  115.5 0.1 copy-done.33
  115.5 28.5 %near_last.1 = f32[3,64,144]{2,1,0:T(8,128)} custom-call(s32[296]{0:T(512)} %copy-done.17, s32[296]{0:T(512)} %copy-done.18, s32[296]{0:T(512)} %copy-done.19, s32[2]{0:T(128)} %copy-done.20, f32[3,64]{1,0:T(4,128)} %bitcast.33, f32[64,8,128]{2,1,0:T(8,128)} %copy-done.26, f32[64,8,128]{2,1,0:T(8,128)} %copy-done.30, f32[64,8,128]{2,1,0:T(8,128)} %copy-done.28, ...), custom_call_target="tpu_custom_call" | custom-call | tf_op jit(solution)/shard_map/near_last/pallas_call | solution.py:398
  (58 shorter events, 0.1 us)
Async XLA Ops:
  0.0 0.9 copy-start.2
  0.9 0.9 copy-start.4
  1.9 0.8 copy-start.11
  2.7 0.7 copy-start.12
  3.4 0.7 copy-start.13
  4.1 0.7 copy-start.22
  4.9 78.8 %copy-start.8 = (f32[512,128]{1,0:T(8,128)}, f32[512,128]{1,0:T(8,128)S(1)}, u32[]{:S(2)}) copy-start(f32[512,128]{1,0:T(8,128)S(1)} %get-tuple-element.23) | copy-start | bytes 786436
  4.9 32.0 %collective-permute-start.9 = (f32[64,8,128]{2,1,0:T(8,128)S(1)}, f32[64,8,128]{2,1,0:T(8,128)S(1)}, u32[]{:S(2)}, u32[]{:S(2)}) collective-permute-start(f32[64,8,128]{2,1,0:T(8,128)S(1)} %bitcast.23), channel_id=1, source_target_pairs={{0,2},{1,3},{2,0},{3,1},{4,6},{5,7},{6,4},{7,5},{8,10},{9,11},{10,... | collective-permute-start | bytes 786440 | tf_op jit(solution)/shard_map/ppermute | solution.py:460
  8.0 29.4 %collective-permute-start.8 = (f32[64,8,128]{2,1,0:T(8,128)S(1)}, f32[64,8,128]{2,1,0:T(8,128)S(1)}, u32[]{:S(2)}, u32[]{:S(2)}) collective-permute-start(f32[64,8,128]{2,1,0:T(8,128)S(1)} %bitcast.24), channel_id=1, source_target_pairs={{0,1},{1,0},{2,3},{3,2},{4,5},{5,4},{6,7},{7,6},{8,9},{9,8},{10,11... | collective-permute-start | bytes 786440 | tf_op jit(solution)/shard_map/ppermute | solution.py:460
  8.0 23.8 %collective-permute-start = (f32[64,8,128]{2,1,0:T(8,128)S(1)}, f32[64,8,128]{2,1,0:T(8,128)S(1)}, u32[]{:S(2)}, u32[]{:S(2)}) collective-permute-start(f32[64,8,128]{2,1,0:T(8,128)S(1)} %bitcast.25), channel_id=1, source_target_pairs={{0,4},{4,8},{8,12},{12,16},{16,20},{20,24},{24,28},{1,5},{5,9},{9,... | collective-permute-start | bytes 786440 | tf_op jit(solution)/shard_map/ppermute | solution.py:495
  11.4 22.0 %collective-permute-start.4 = (f32[64,8,128]{2,1,0:T(8,128)S(1)}, f32[64,8,128]{2,1,0:T(8,128)S(1)}, u32[]{:S(2)}, u32[]{:S(2)}) collective-permute-start(f32[64,8,128]{2,1,0:T(8,128)S(1)} %bitcast.26), channel_id=1, source_target_pairs={{4,0},{8,4},{12,8},{16,12},{20,16},{24,20},{28,24},{5,1},{9,5},{13... | collective-permute-start | bytes 786440 | tf_op jit(solution)/shard_map/ppermute | solution.py:494
  12.7 11.2 %collective-permute-start.11 = (f32[1,8,128]{2,1,0:T(8,128)S(1)}, f32[1,8,128]{2,1,0:T(8,128)S(1)}, u32[]{:S(2)}, u32[]{:S(2)}) collective-permute-start(f32[1,8,128]{2,1,0:T(8,128)S(1)} %bitcast.28), channel_id=1, source_target_pairs={{0,16},{4,20},{8,24},{12,28},{16,0},{20,4},{24,8},{28,12},{1,17},{... | collective-permute-start | bytes 12296 | tf_op jit(solution)/shard_map/ppermute | solution.py:460
  23.8 3.7 %collective-permute-start.12 = (f32[2,8,128]{2,1,0:T(8,128)S(1)}, f32[2,8,128]{2,1,0:T(8,128)S(1)}, u32[]{:S(2)}, u32[]{:S(2)}) collective-permute-start(f32[2,8,128]{2,1,0:T(8,128)S(1)} %pad_maximum_fusion.2), channel_id=1, source_target_pairs={{0,8},{4,12},{8,0},{12,4},{16,24},{20,28},{24,16},{28,20},{1,9},{5... | collective-permute-start | bytes 24584 | tf_op jit(solution)/shard_map/ppermute | solution.py:460
  27.5 3.7 %collective-permute-start.13 = (f32[4,8,128]{2,1,0:T(8,128)S(1)}, f32[4,8,128]{2,1,0:T(8,128)S(1)}, u32[]{:S(2)}, u32[]{:S(2)}) collective-permute-start(f32[4,8,128]{2,1,0:T(8,128)S(1)} %pad_maximum_fusion.1), channel_id=1, source_target_pairs={{0,4},{4,0},{8,12},{12,8},{16,20},{20,16},{24,28},{28,24},{1,5},{5... | collective-permute-start | bytes 49160 | tf_op jit(solution)/shard_map/ppermute | solution.py:460
  31.2 4.3 %collective-permute-start.14 = (f32[8,8,128]{2,1,0:T(8,128)S(1)}, f32[8,8,128]{2,1,0:T(8,128)S(1)}, u32[]{:S(2)}, u32[]{:S(2)}) collective-permute-start(f32[8,8,128]{2,1,0:T(8,128)S(1)} %pad_maximum_fusion), channel_id=1, source_target_pairs={{0,2},{1,3},{2,0},{3,1},{4,6},{5,7},{6,4},{7,5},{8,10},{9,11},{10,... | collective-permute-start | bytes 98312 | tf_op jit(solution)/shard_map/ppermute | solution.py:460
  31.7 82.8 %copy-start.26 = (f32[64,8,128]{2,1,0:T(8,128)}, f32[64,8,128]{2,1,0:T(8,128)S(1)}, u32[]{:S(2)}) copy-start(f32[64,8,128]{2,1,0:T(8,128)S(1)} %collective-permute-done.refs_5_) | copy-start | bytes 786436
  31.8 8.0 %collective-permute-start.2 = (f32[64,8,128]{2,1,0:T(8,128)S(1)}, f32[64,8,128]{2,1,0:T(8,128)S(1)}, u32[]{:S(2)}, u32[]{:S(2)}) collective-permute-start(f32[64,8,128]{2,1,0:T(8,128)S(1)} %collective-permute-done.refs_5_), channel_id=1, source_target_pairs={{0,2},{1,3},{2,0},{3,1},{4,6},{5,7},{6,4},{7,5},{8,10},{9,11},{10,... | collective-permute-start | bytes 786440 | tf_op jit(solution)/shard_map/ppermute | solution.py:460
  33.3 81.3 %copy-start.27 = (f32[64,8,128]{2,1,0:T(8,128)}, f32[64,8,128]{2,1,0:T(8,128)S(1)}, u32[]{:S(2)}) copy-start(f32[64,8,128]{2,1,0:T(8,128)S(1)} %collective-permute-done.4.refs_9_) | copy-start | bytes 786436
  33.3 9.2 %collective-permute-start.6 = (f32[64,8,128]{2,1,0:T(8,128)S(1)}, f32[64,8,128]{2,1,0:T(8,128)S(1)}, u32[]{:S(2)}, u32[]{:S(2)}) collective-permute-start(f32[64,8,128]{2,1,0:T(8,128)S(1)} %collective-permute-done.4.refs_9_), channel_id=1, source_target_pairs={{0,2},{1,3},{2,0},{3,1},{4,6},{5,7},{6,4},{7,5},{8,10},{9,11},{10,... | collective-permute-start | bytes 786440 | tf_op jit(solution)/shard_map/ppermute | solution.py:460
  35.6 1.3 collective-permute-start.15
  36.8 77.7 %collective-permute-start.1 = (f32[64,8,128]{2,1,0:T(8,128)S(1)}, f32[64,8,128]{2,1,0:T(8,128)S(1)}, u32[]{:S(2)}, u32[]{:S(2)}) collective-permute-start(f32[64,8,128]{2,1,0:T(8,128)S(1)} %collective-permute-done.refs_5_), channel_id=1, source_target_pairs={{0,1},{1,0},{2,3},{3,2},{4,5},{5,4},{6,7},{7,6},{8,9},{9,8},{10,11... | collective-permute-start | bytes 786440 | tf_op jit(solution)/shard_map/ppermute | solution.py:460
  37.0 46.7 %copy-start.23 = (f32[64,8,128]{2,1,0:T(8,128)}, f32[64,8,128]{2,1,0:T(8,128)S(1)}, u32[]{:S(2)}) copy-start(f32[64,8,128]{2,1,0:T(8,128)S(1)} %collective-permute-done.9.refs_7_) | copy-start | bytes 786436
  37.0 77.5 %collective-permute-start.5 = (f32[64,8,128]{2,1,0:T(8,128)S(1)}, f32[64,8,128]{2,1,0:T(8,128)S(1)}, u32[]{:S(2)}, u32[]{:S(2)}) collective-permute-start(f32[64,8,128]{2,1,0:T(8,128)S(1)} %collective-permute-done.4.refs_9_), channel_id=1, source_target_pairs={{0,1},{1,0},{2,3},{3,2},{4,5},{5,4},{6,7},{7,6},{8,9},{9,8},{10,11... | collective-permute-start | bytes 786440 | tf_op jit(solution)/shard_map/ppermute | solution.py:460
  37.3 46.4 %copy-start.24 = (f32[64,8,128]{2,1,0:T(8,128)}, f32[64,8,128]{2,1,0:T(8,128)S(1)}, u32[]{:S(2)}) copy-start(f32[64,8,128]{2,1,0:T(8,128)S(1)} %collective-permute-done.8.refs_6_) | copy-start | bytes 786436
  37.3 46.4 %collective-permute-start.10 = (f32[64,8,128]{2,1,0:T(8,128)S(1)}, f32[64,8,128]{2,1,0:T(8,128)S(1)}, u32[]{:S(2)}, u32[]{:S(2)}) collective-permute-start(f32[64,8,128]{2,1,0:T(8,128)S(1)} %collective-permute-done.9.refs_7_), channel_id=1, source_target_pairs={{0,1},{1,0},{2,3},{3,2},{4,5},{5,4},{6,7},{7,6},{8,9},{9,8},{10,11... | collective-permute-start | bytes 786440 | tf_op jit(solution)/shard_map/ppermute | solution.py:460
  39.8 74.8 %copy-start.28 = (f32[64,8,128]{2,1,0:T(8,128)}, f32[64,8,128]{2,1,0:T(8,128)S(1)}, u32[]{:S(2)}) copy-start(f32[64,8,128]{2,1,0:T(8,128)S(1)} %collective-permute-done.2.refs_7_) | copy-start | bytes 786436
  39.8 74.8 %collective-permute-start.3 = (f32[64,8,128]{2,1,0:T(8,128)S(1)}, f32[64,8,128]{2,1,0:T(8,128)S(1)}, u32[]{:S(2)}, u32[]{:S(2)}) collective-permute-start(f32[64,8,128]{2,1,0:T(8,128)S(1)} %collective-permute-done.2.refs_7_), channel_id=1, source_target_pairs={{0,1},{1,0},{2,3},{3,2},{4,5},{5,4},{6,7},{7,6},{8,9},{9,8},{10,11... | collective-permute-start | bytes 786440 | tf_op jit(solution)/shard_map/ppermute | solution.py:460
  42.6 72.0 %copy-start.29 = (f32[64,8,128]{2,1,0:T(8,128)}, f32[64,8,128]{2,1,0:T(8,128)S(1)}, u32[]{:S(2)}) copy-start(f32[64,8,128]{2,1,0:T(8,128)S(1)} %collective-permute-done.6.refs_11_) | copy-start | bytes 786436
  42.6 72.0 %collective-permute-start.7 = (f32[64,8,128]{2,1,0:T(8,128)S(1)}, f32[64,8,128]{2,1,0:T(8,128)S(1)}, u32[]{:S(2)}, u32[]{:S(2)}) collective-permute-start(f32[64,8,128]{2,1,0:T(8,128)S(1)} %collective-permute-done.6.refs_11_), channel_id=1, source_target_pairs={{0,1},{1,0},{2,3},{3,2},{4,5},{5,4},{6,7},{7,6},{8,9},{9,8},{10,11... | collective-permute-start | bytes 786440 | tf_op jit(solution)/shard_map/ppermute | solution.py:460
  43.5 0.9 copy-start.3
  44.4 0.9 copy-start.5
  45.3 1.0 copy-start.7
  46.3 0.9 copy-start.10
  47.2 0.7 copy-start.21
  70.8 3.6 %copy-start = (bf16[64,4,144,128]{3,2,1,0:T(8,128)(2,1)}, bf16[64,4,144,128]{3,2,1,0:T(8,128)(2,1)S(1)}, u32[]{:S(2)}) copy-start(bf16[64,4,144,128]{3,2,1,0:T(8,128)(2,1)S(1)} %get-tuple-element.24.refs_9_.refs_13_) | copy-start | bytes 28311556
  74.4 0.9 copy-start.1
  75.4 0.7 copy-start.9
  76.1 0.6 copy-start.17
  76.7 0.6 copy-start.18
  77.2 0.6 copy-start.19
  77.8 0.6 copy-start.20
  78.4 0.6 copy-start.14
  78.4 0.6 copy-start.15
  78.4 0.6 copy-start.16
  83.1 0.6 copy-start.6
  83.7 0.7 copy-start.25
  114.5 0.7 copy-start.30
  114.5 0.8 copy-start.31
  114.6 0.9 copy-start.32
  114.6 1.0 copy-start.33
